TPU v7x, 32 devices: a whole 2x2x4 slice. The times are simulated.
32 devices in a mesh: job: 2 (over x), unit: 16 (over z, y, core).
Axes of the slice: x: 2, y: 2, z: 4, core: 2. Of those that a mesh axis runs over, the one named last changes fastest.
Arguments:
- query_grad: bfloat16 [16384, 28672], P('job', 'unit'), parts along dimension 0, may hold values from -0.00036621094 to 0.00036621094
- out_grads: bfloat16 [512, 8192], P(('job', 'unit')), parts along dimension 0, may hold values from -6 to 6
- inputs: bfloat16 [512, 28672], P('job', 'unit'), parts along dimension 0, may hold values from -6 to 6
Outputs:
- scores: float32 [512], P('job'), parts along dimension 0
There are 2 independent parts, one for each index of `job`. A program takes and returns all parts, laid end to end along the dimension named above; each array names one. Nothing has to cross between parts.
All inputs are finite; a program needn't handle non-finite values.
Results may differ from a plain program's by a relative error of at most 0.0003.
Values may be sent and summed in bfloat16 or wider, within the bound.
No kernel may reach another device: no remote copies, remote signals or barrier semaphores. Data moves between devices by JAX's collectives and lax.ppermute only.
A program may use at most 128 MiB of HBM per device.

v0:
```python
import jax
import jax.numpy as jnp
from jax import lax
from jax.sharding import PartitionSpec as P


def body(query_grad, out_grads, inputs):
    projected = jnp.dot(
        lax.all_gather(out_grads, "unit", axis=0, tiled=True),
        query_grad,
        preferred_element_type=jnp.float32,
    )
    partial_value = jnp.sum(projected * inputs.astype(jnp.float32), axis=1)
    return lax.psum(partial_value, "unit")


def solution(mesh):
    return jax.shard_map(
        body,
        mesh=mesh,
        in_specs=(P("job", "unit"), P(("job", "unit"), None), P("job", "unit")),
        out_specs=P("job"),
        check_vma=False,
    )
```

profile of v0, /device:TPU:0, one launch (start us, length us, event | category | flops | bytes accessed | tf_op | source)
XLA Modules:
  0.0 116.4 jit_solution(11563475330137340531)
XLA Ops:
  6.5 0.0 all-gather.2.cloned.1.call-start
  6.5 0.7 all-gather.2.cloned.1.call-update
  7.3 55.6 %all-gather.2.cloned.1.call-done = bf16[256,8192]{1,0:T(8,128)(2,1)} async-done(((bf16[16,8192]{1,0:T(8,128)(2,1)}), bf16[256,8192]{1,0:T(8,128)(2,1)}) %all-gather.2.cloned.1.call-update) | async-done | bytes 4194320 | tf_op jit(solution)/shard_map/all_gather | solution.py:9
  62.8 15.0 %fusion = f32[256]{0:T(256)S(1)} fusion(bf16[256,1792]{1,0:T(8,128)(2,1)} %param.5, bf16[256,8192]{1,0:T(8,128)(2,1)} %all-gather.2.cloned.1.call-done, bf16[8192,1792]{1,0:T(8,128)(2,1)} %param.3), kind=kOutput, calls=%fused_computation.1 | convolution fusion | flops 7517569024 | bytes 34472960 | tf_op jit(solution)/shard_map/dot_general | solution.py:8
  77.9 31.7 %psum.7 = f32[256]{0:T(256)} all-reduce(f32[256]{0:T(256)S(1)} %fusion), channel_id=1, replica_groups=mesh['job'=2,'unit'=16] {'unit'}, use_global_device_ids=true, to_apply=%region_1.0 | all-reduce | flops 256 | bytes 2048 | tf_op jit(solution)/shard_map/psum | solution.py:14
Async XLA Ops:
  6.5 56.3 %all-gather.2.cloned.1.call-start = ((), (), s32[]{:S(2)}) async-start(), calls=%async_computation | async-start | bytes 4456448 | tf_op jit(solution)/shard_map/all_gather | solution.py:9
Sparse Core Ops, SparseCore 0:
  9.5 53.2 all-gather.1
where the time goes:
time: 117 us; the launch traced here: 116 us
  waiting for transfers between devices  56.3 us (48%)
  blocking collectives  31.7 us (27%)
  matrix products  15 us (13%)
  between operations  13.4 us (11%)
    all_gather x1, waiting for transfers between devices, body(): lax.all_gather(out_grads, 'unit', axis=0, tiled=True)  55.6 us
    psum x1, blocking collectives, body(): return lax.psum(partial_value, 'unit')  31.7 us
    dot_general x1, matrix products, body(): jnp.dot(lax.all_gather(out_grads, 'unit', axis=0, tiled=True), query_grad...  15 us
  transfers between devices with their start and end apart: 1, of which 1 were waited for; matrix products, arithmetic and copies ran while one was open for 0% of the time, Pallas kernels for 0%

commit v1 on v0

v1 whole, which is shorter than its diff:
```python
import functools

import jax
import jax.numpy as jnp
import numpy as np
from jax import lax
from jax.experimental import pallas as pl
from jax.experimental.pallas import tpu as pltpu
from jax.sharding import PartitionSpec as P

PIECES = 4
STEP = 1024
LANES = 128
VMEM = pl.BlockSpec(memory_space=pltpu.VMEM)


def ring_of(units):
    chips = units // 2
    if units != 16:
        return [2 * chip for chip in range(chips)]
    there = [2 * chip for chip in range(0, chips, 2)]
    return there + [2 * chip for chip in range(chips - 1, 0, -2)]


def plan(units):
    ring = ring_of(units)
    chips = len(ring)
    at = lambda place, core: ring[place % chips] + core
    ahead, across, twin = [], [], []
    held = np.zeros((units, chips), np.int32)
    for place in range(chips):
        for core, way in ((0, 1), (1, -1)):
            me = at(place, core)
            ahead.append((me, at(place + way, core)))
            across.append((at(place, 1 - core), at(place + way, core)))
            twin.append((me, at(place, 1 - core)))
            blocks = [me]
            for hop in range(1, chips // 2):
                blocks += [at(place - way * hop, core), at(place - way * hop, 1 - core)]
            blocks.append(at(place - way * (chips // 2), core))
            held[me] = blocks
    other = np.array([dict(twin)[unit] for unit in range(units)])
    return ahead, across, twin, np.concatenate([held, held[other]], axis=1)


def weigh_kernel(first, order, x_ref, q_ref, keep_ref, send_ref, rows):
    block = x_ref.shape[0] // order.shape[0]
    for place in range(order.shape[0]):
        start = pl.multiple_of(order[place] * block, block)
        rows[place * block : (place + 1) * block, :] = x_ref[pl.ds(start, block), :]
    half = keep_ref.shape[0]
    step = min(STEP, keep_ref.shape[1])

    @pl.loop(0, keep_ref.shape[1] // step)
    def _(i):
        at = pl.multiple_of(i * step, step)
        value = lax.dot_general(
            rows[...],
            q_ref[pl.ds(first + at, step), :],
            (((1,), (1,)), ((), ())),
            preferred_element_type=jnp.float32,
        )
        keep_ref[:, pl.ds(at, step)] = value[:half]
        send_ref[:, pl.ds(at, step)] = value[half:]


def weigh(first, width, order, x, q):
    tokens, depth = x.shape
    half = jax.ShapeDtypeStruct((tokens // 2, width), jnp.float32)
    return pl.pallas_call(
        functools.partial(weigh_kernel, first),
        in_specs=[pl.BlockSpec(memory_space=pltpu.SMEM), VMEM, VMEM],
        out_specs=[VMEM, VMEM],
        out_shape=[pltpu.VMEM(half.shape, half.dtype), half],
        scratch_shapes=[pltpu.VMEM((tokens, depth), x.dtype)],
        compiler_params=pltpu.CompilerParams(vmem_limit_bytes=12 << 20),
        cost_estimate=pl.CostEstimate(
            flops=2 * tokens * depth * width,
            bytes_accessed=2 * depth * width,
            transcendentals=0,
        ),
    )(order, x, q)


def dots(gradient, row, mine, theirs):
    block = gradient.shape[0]
    total = jnp.zeros((block, LANES), jnp.float32)
    width = mine[0].shape[1]
    for piece in range(len(mine)):
        for lane in range(0, width, LANES):
            weight = (
                mine[piece][row : row + block, lane : lane + LANES]
                + theirs[piece][row : row + block, lane : lane + LANES]
            )
            at = piece * width + lane
            total += gradient[:, at : at + LANES].astype(jnp.float32) * weight
    return total


def early_kernel(count, *refs):
    gradients, mine, theirs = refs[:count], refs[count : count + PIECES], refs[count + PIECES : -1]
    block = gradients[0].shape[0]
    for index in range(count):
        refs[-1][index * block : (index + 1) * block, :] = dots(
            gradients[index], index * block, mine, theirs
        )


def last_kernel(order, gradient, *refs):
    early, out, table = refs[-3:]
    mine, theirs = refs[:PIECES], refs[PIECES : 2 * PIECES]
    block = gradient.shape[0]
    blocks = early.shape[0] // block
    table[...] = jnp.zeros_like(table)
    for place in range(blocks):
        start = pl.multiple_of(order[place] * block, block)
        table[pl.ds(start, block), :] = early[place * block : (place + 1) * block, :]
    start = pl.multiple_of(order[blocks] * block, block)
    table[pl.ds(start, block), :] = dots(gradient, blocks * block, mine, theirs)
    out[...] = jnp.sum(table[...].T, axis=0, keepdims=True)


def in_vmem(arrays):
    return [pltpu.with_memory_space_constraint(array, pltpu.VMEM) for array in arrays]


def body(units, query_grad, out_grads, inputs):
    ahead, across, twin, orders = plan(units)
    send = lambda value, pairs: lax.ppermute(value, "unit", pairs)
    order = jnp.asarray(orders)[lax.axis_index("unit")]
    tokens = inputs.shape[0]
    block = out_grads.shape[0]
    width = query_grad.shape[0] // PIECES

    held = [out_grads, send(out_grads, ahead), send(out_grads, across)]
    for hop in range(2, units // 4):
        held += [send(held[-2], ahead), send(held[-1], ahead)]
    last = send(held[-2], ahead)

    q = pltpu.with_memory_space_constraint(query_grad, pltpu.VMEM)
    mine, theirs = [], []
    for piece in range(PIECES):
        keep, give = weigh(piece * width, width, order, inputs, q)
        mine.append(keep)
        theirs.append(send(give, twin))

    early = pl.pallas_call(
        functools.partial(early_kernel, len(held)),
        in_specs=[VMEM] * (len(held) + 2 * PIECES),
        out_specs=VMEM,
        out_shape=jax.ShapeDtypeStruct((len(held) * block, LANES), jnp.float32),
        compiler_params=pltpu.CompilerParams(vmem_limit_bytes=12 << 20),
    )(*held, *in_vmem(mine), *in_vmem(theirs))
    partial_value = pl.pallas_call(
        last_kernel,
        in_specs=[pl.BlockSpec(memory_space=pltpu.SMEM)] + [VMEM] * (2 + 2 * PIECES),
        out_specs=VMEM,
        out_shape=jax.ShapeDtypeStruct((1, tokens), jnp.float32),
        scratch_shapes=[pltpu.VMEM((tokens, LANES), jnp.float32)],
        compiler_params=pltpu.CompilerParams(vmem_limit_bytes=12 << 20),
    )(order, last, *in_vmem(mine), *in_vmem(theirs), early)

    bit = 1
    while bit < units:
        pairs = [(unit, unit ^ bit) for unit in range(units)]
        partial_value += send(partial_value, pairs)
        bit *= 2
    return partial_value.reshape(tokens)


def solution(mesh):
    return jax.shard_map(
        functools.partial(body, mesh.shape["unit"]),
        mesh=mesh,
        in_specs=(P("job", "unit"), P(("job", "unit"), None), P("job", "unit")),
        out_specs=P("job"),
        check_vma=False,
    )
```

time: 117 us -> 69.8 us (0.60)
  blocking collectives: 31.7 us -> 0 us
  waiting for transfers between devices: 56.3 us -> 28.1 us
  starting transfers between devices: 0.01 us -> 16.7 us
  matrix products: 15 us -> 0 us
  between operations: 13.4 us -> 0.11 us
  Pallas kernels: 0 us -> 12.9 us
  local copies, waits for them, and re-layouts: 0 us -> 11.2 us
    all_gather x1 -> x0, waiting for transfers between devices: 55.6 us -> none  [body(): lax.all_gather(out_grads, 'unit', axis=0, tiled=True)]
    psum x1 -> x0, blocking collectives: 31.7 us -> none  [body(): return lax.psum(partial_value, 'unit')]
    ppermute x0 -> x15, waiting for transfers between devices: none -> 28.1 us  [body(): send = lambda value, pairs: lax.ppermute(value, 'unit', pairs)]
    ppermute x0 -> x15, starting transfers between devices: none -> 16.7 us  [body(): send = lambda value, pairs: lax.ppermute(value, 'unit', pairs)]
    dot_general x1 -> x0, matrix products: 15 us -> none  [body(): jnp.dot(lax.all_gather(out_grads, 'unit', axis=0, tiled=True), query_grad...]
    pallas_call x0 -> x6, Pallas kernels: none -> 12.9 us  [the longest x4 11.6 us: weigh(): pl.pallas_call(functools.partial(weigh_kernel, first), in_specs=[pl.Block...]
    unnamed x0 -> x6, local copies, waits for them, and re-layouts: none -> 10.5 us
  transfers between devices with their start and end apart: 1 -> 15, of which waited for: 1 -> 8; matrix products, arithmetic and copies ran while one was open for 0% -> 1% of each run, Pallas kernels for 0% -> 17%
where the time goes in v1:
time: 69.8 us; the launch traced here: 69.6 us
  waiting for transfers between devices  28.1 us (40%)
  starting transfers between devices  16.7 us (24%)
  Pallas kernels  12.9 us (18%)
  local copies, waits for them, and re-layouts  11.2 us (16%)
    ppermute x15, waiting for transfers between devices, body(): send = lambda value, pairs: lax.ppermute(value, 'unit', pairs)  28.1 us
    ppermute x15, starting transfers between devices, body(): send = lambda value, pairs: lax.ppermute(value, 'unit', pairs)  16.7 us
    pallas_call x4, Pallas kernels, weigh(): pl.pallas_call(functools.partial(weigh_kernel, first), in_specs=[pl.Block...  11.6 us
    unnamed x6, local copies, waits for them, and re-layouts  10.5 us
  transfers between devices with their start and end apart: 15, of which 8 were waited for; matrix products, arithmetic and copies ran while one was open for 1% of the time, Pallas kernels for 17%

profile of v1, /device:TPU:0, one launch (start us, length us, event | category | flops | bytes accessed | tf_op | source)
XLA Modules:
  0.0 69.6 jit_solution(15994202772747573108)
XLA Ops:
  0.0 3.0 %collective-permute-start = (bf16[16,8192]{1,0:T(8,128)(2,1)}, bf16[16,8192]{1,0:T(8,128)(2,1)S(1)}, u32[]{:S(2)}, u32[]{:S(2)}) collective-permute-start(bf16[16,8192]{1,0:T(8,128)(2,1)} %refs_0_.1), channel_id=1, source_target_pairs={{0,4},{1,3},{4,8},{5,1},{8,12},{9,5},{12,14},{13,9},{14,10},{15,13... | collective-permute-start | bytes 786440 | tf_op jit(solution)/shard_map/ppermute | solution.py:129
  3.0 0.7 collective-permute-start.8
  3.7 0.7 dynamic-slice_bitcast_fusion.order
  4.4 0.0 copy-start
  4.4 9.3 %copy-done = bf16[8192,1792]{1,0:T(8,128)(2,1)S(1)} copy-done((bf16[8192,1792]{1,0:T(8,128)(2,1)S(1)}, bf16[8192,1792]{1,0:T(8,128)(2,1)}, u32[]{:S(2)}) %copy-start) | copy-done | bytes 29360152
  13.7 0.0 copy-start.1
  13.7 1.2 %copy-done.1 = bf16[256,1792]{1,0:T(8,128)(2,1)S(1)} copy-done((bf16[256,1792]{1,0:T(8,128)(2,1)S(1)}, bf16[256,1792]{1,0:T(8,128)(2,1)}, u32[]{:S(2)}) %copy-start.1) | copy-done | bytes 917528
  14.9 2.9 %shard_map.46 = (f32[128,2048]{1,0:T(8,128)S(1)}, f32[128,2048]{1,0:T(8,128)S(1)}) custom-call(s32[16]{0:T(128)S(1)} %dynamic-slice_bitcast_fusion.order, bf16[256,1792]{1,0:T(8,128)(2,1)S(1)} %copy-done.1, bf16[8192,1792]{1,0:T(8,128)(2,1)S(1)} %copy-done), custom_call_target="tpu_custom_call" | custom-call | flops 1879048192 | bytes 7340032 | tf_op jit(solution)/shard_map/pallas_call | solution.py:70
  17.8 1.1 %collective-permute-start.4 = (f32[128,2048]{1,0:T(8,128)S(1)}, f32[128,2048]{1,0:T(8,128)S(1)}, u32[]{:S(2)}, u32[]{:S(2)}) collective-permute-start(f32[128,2048]{1,0:T(8,128)S(1)} %get-tuple-element.17), channel_id=1, source_target_pairs={{0,1},{1,0},{4,5},{5,4},{8,9},{9,8},{12,13},{13,12},{14,15},{15,14... | collective-permute-start | bytes 3145736 | tf_op jit(solution)/shard_map/ppermute | solution.py:129
  18.9 2.9 %shard_map.47 = (f32[128,2048]{1,0:T(8,128)S(1)}, f32[128,2048]{1,0:T(8,128)S(1)}) custom-call(s32[16]{0:T(128)S(1)} %dynamic-slice_bitcast_fusion.order, bf16[256,1792]{1,0:T(8,128)(2,1)S(1)} %copy-done.1, bf16[8192,1792]{1,0:T(8,128)(2,1)S(1)} %copy-done), custom_call_target="tpu_custom_call" | custom-call | flops 1879048192 | bytes 7340032 | tf_op jit(solution)/shard_map/pallas_call | solution.py:70
  21.8 0.0 copy-start.2
  21.8 0.1 collective-permute-start.5
  21.9 0.0 collective-permute-done.refs_1_
  21.9 1.6 %collective-permute-start.1 = (bf16[16,8192]{1,0:T(8,128)(2,1)S(1)}, bf16[16,8192]{1,0:T(8,128)(2,1)S(1)}, u32[]{:S(2)}, u32[]{:S(2)}) collective-permute-start(bf16[16,8192]{1,0:T(8,128)(2,1)S(1)} %collective-permute-done.refs_1_), channel_id=1, source_target_pairs={{0,4},{1,3},{4,8},{5,1},{8,12},{9,5},{12,14},{13,9},{14,10},{15,13... | collective-permute-start | bytes 786440 | tf_op jit(solution)/shard_map/ppermute | solution.py:129
  23.5 2.9 %shard_map.48 = (f32[128,2048]{1,0:T(8,128)S(1)}, f32[128,2048]{1,0:T(8,128)S(1)}) custom-call(s32[16]{0:T(128)S(1)} %dynamic-slice_bitcast_fusion.order, bf16[256,1792]{1,0:T(8,128)(2,1)S(1)} %copy-done.1, bf16[8192,1792]{1,0:T(8,128)(2,1)S(1)} %copy-done), custom_call_target="tpu_custom_call" | custom-call | flops 1879048192 | bytes 7340032 | tf_op jit(solution)/shard_map/pallas_call | solution.py:70
  26.4 0.1 collective-permute-start.6
  26.5 2.9 %shard_map.49 = (f32[128,2048]{1,0:T(8,128)S(1)}, f32[128,2048]{1,0:T(8,128)S(1)}) custom-call(s32[16]{0:T(128)S(1)} %dynamic-slice_bitcast_fusion.order, bf16[256,1792]{1,0:T(8,128)(2,1)S(1)} %copy-done.1, bf16[8192,1792]{1,0:T(8,128)(2,1)S(1)} %copy-done), custom_call_target="tpu_custom_call" | custom-call | flops 1879048192 | bytes 7340032 | tf_op jit(solution)/shard_map/pallas_call | solution.py:70
  29.4 0.0 collective-permute-done.8.refs_2_
  29.4 0.6 collective-permute-start.7
  30.0 0.0 collective-permute-done.1.refs_3_
  30.0 1.5 %collective-permute-start.9 = (bf16[16,8192]{1,0:T(8,128)(2,1)S(1)}, bf16[16,8192]{1,0:T(8,128)(2,1)S(1)}, u32[]{:S(2)}, u32[]{:S(2)}) collective-permute-start(bf16[16,8192]{1,0:T(8,128)(2,1)S(1)} %collective-permute-done.8.refs_2_), channel_id=1, source_target_pairs={{0,4},{1,3},{4,8},{5,1},{8,12},{9,5},{12,14},{13,9},{14,10},{15,13... | collective-permute-start | bytes 786440 | tf_op jit(solution)/shard_map/ppermute | solution.py:129
  31.5 4.8 %collective-permute-done.9.refs_4_ = bf16[16,8192]{1,0:T(8,128)(2,1)S(1)} collective-permute-done((bf16[16,8192]{1,0:T(8,128)(2,1)S(1)}, bf16[16,8192]{1,0:T(8,128)(2,1)S(1)}, u32[]{:S(2)}, u32[]{:S(2)}) %collective-permute-start.9) | collective-permute-done | bytes 262176 | tf_op jit(solution)/shard_map/ppermute | solution.py:129
  36.4 1.5 %collective-permute-start.2 = (bf16[16,8192]{1,0:T(8,128)(2,1)S(1)}, bf16[16,8192]{1,0:T(8,128)(2,1)S(1)}, u32[]{:S(2)}, u32[]{:S(2)}) collective-permute-start(bf16[16,8192]{1,0:T(8,128)(2,1)S(1)} %collective-permute-done.1.refs_3_), channel_id=1, source_target_pairs={{0,4},{1,3},{4,8},{5,1},{8,12},{9,5},{12,14},{13,9},{14,10},{15,13... | collective-permute-start | bytes 786440 | tf_op jit(solution)/shard_map/ppermute | solution.py:129
  37.9 4.8 %collective-permute-done.2.refs_5_ = bf16[16,8192]{1,0:T(8,128)(2,1)S(1)} collective-permute-done((bf16[16,8192]{1,0:T(8,128)(2,1)S(1)}, bf16[16,8192]{1,0:T(8,128)(2,1)S(1)}, u32[]{:S(2)}, u32[]{:S(2)}) %collective-permute-start.2) | collective-permute-done | bytes 262176 | tf_op jit(solution)/shard_map/ppermute | solution.py:129
  42.7 1.5 %collective-permute-start.10 = (bf16[16,8192]{1,0:T(8,128)(2,1)S(1)}, bf16[16,8192]{1,0:T(8,128)(2,1)S(1)}, u32[]{:S(2)}, u32[]{:S(2)}) collective-permute-start(bf16[16,8192]{1,0:T(8,128)(2,1)S(1)} %collective-permute-done.9.refs_4_), channel_id=1, source_target_pairs={{0,4},{1,3},{4,8},{5,1},{8,12},{9,5},{12,14},{13,9},{14,10},{15,13... | collective-permute-start | bytes 786440 | tf_op jit(solution)/shard_map/ppermute | solution.py:129
  44.2 4.8 %collective-permute-done.10.refs_6_ = bf16[16,8192]{1,0:T(8,128)(2,1)S(1)} collective-permute-done((bf16[16,8192]{1,0:T(8,128)(2,1)S(1)}, bf16[16,8192]{1,0:T(8,128)(2,1)S(1)}, u32[]{:S(2)}, u32[]{:S(2)}) %collective-permute-start.10) | collective-permute-done | bytes 262176 | tf_op jit(solution)/shard_map/ppermute | solution.py:129
  49.1 1.5 %collective-permute-start.3 = (bf16[16,8192]{1,0:T(8,128)(2,1)S(1)}, bf16[16,8192]{1,0:T(8,128)(2,1)S(1)}, u32[]{:S(2)}, u32[]{:S(2)}) collective-permute-start(bf16[16,8192]{1,0:T(8,128)(2,1)S(1)} %collective-permute-done.2.refs_5_), channel_id=1, source_target_pairs={{0,4},{1,3},{4,8},{5,1},{8,12},{9,5},{12,14},{13,9},{14,10},{15,13... | collective-permute-start | bytes 786440 | tf_op jit(solution)/shard_map/ppermute | solution.py:129
  50.6 0.0 collective-permute-done.4.refs_11_.refs_4_
  50.6 0.0 collective-permute-done.5.refs_12_.refs_5_
  50.6 0.0 collective-permute-done.6.refs_13_.refs_6_
  50.6 0.0 collective-permute-done.7.refs_14_.refs_7_
  50.6 0.0 copy-done.2
  50.7 0.6 shard_map.50.refs_8_
  51.2 4.2 %collective-permute-done.3.gradient = bf16[16,8192]{1,0:T(8,128)(2,1)S(1)} collective-permute-done((bf16[16,8192]{1,0:T(8,128)(2,1)S(1)}, bf16[16,8192]{1,0:T(8,128)(2,1)S(1)}, u32[]{:S(2)}, u32[]{:S(2)}) %collective-permute-start.3) | collective-permute-done | bytes 262176 | tf_op jit(solution)/shard_map/ppermute | solution.py:129
  55.5 0.7 %shard_map.51 = f32[1,256]{1,0:T(1,128)S(1)} custom-call(s32[16]{0:T(128)S(1)} %dynamic-slice_bitcast_fusion.order, bf16[16,8192]{1,0:T(8,128)(2,1)S(1)} %collective-permute-done.3.gradient, f32[128,2048]{1,0:T(8,128)S(1)} %get-tuple-element.13.refs_7_.refs_0_, f32[128,2048]{1,0:T(8,128)S(1)} %get-tuple-element.14.refs_8_.refs_1_, ...), custom_call_target="tpu_custom_call" | custom-call | tf_op jit(solution)/shard_map/pallas_call | solution.py:154
  56.2 0.1 collective-permute-start.11
  56.3 1.1 %collective-permute-done.11 = f32[1,256]{1,0:T(1,128)S(1)} collective-permute-done((f32[1,256]{1,0:T(1,128)S(1)}, f32[1,256]{1,0:T(1,128)S(1)}, u32[]{:S(2)}, u32[]{:S(2)}) %collective-permute-start.11) | collective-permute-done | bytes 1056 | tf_op jit(solution)/shard_map/ppermute | solution.py:129
  57.4 0.5 collective-permute-start.12
  57.9 3.1 %collective-permute-done.12 = f32[1,256]{1,0:T(1,128)S(1)} collective-permute-done((f32[1,256]{1,0:T(1,128)S(1)}, f32[1,256]{1,0:T(1,128)S(1)}, u32[]{:S(2)}, u32[]{:S(2)}) %collective-permute-start.12) | collective-permute-done | bytes 1056 | tf_op jit(solution)/shard_map/ppermute | solution.py:129
  61.0 1.5 %collective-permute-start.13 = (f32[1,256]{1,0:T(1,128)S(1)}, f32[1,256]{1,0:T(1,128)S(1)}, u32[]{:S(2)}, u32[]{:S(2)}) collective-permute-start(f32[1,256]{1,0:T(1,128)S(1)} %add.17), channel_id=1, source_target_pairs={{0,4},{1,5},{2,6},{3,7},{4,0},{5,1},{6,2},{7,3},{8,12},{9,13},{10,... | collective-permute-start | bytes 3080 | tf_op jit(solution)/shard_map/ppermute | solution.py:129
  62.5 2.0 %collective-permute-done.13 = f32[1,256]{1,0:T(1,128)S(1)} collective-permute-done((f32[1,256]{1,0:T(1,128)S(1)}, f32[1,256]{1,0:T(1,128)S(1)}, u32[]{:S(2)}, u32[]{:S(2)}) %collective-permute-start.13) | collective-permute-done | bytes 1056 | tf_op jit(solution)/shard_map/ppermute | solution.py:129
  64.6 1.4 %collective-permute-start.14 = (f32[1,256]{1,0:T(1,128)S(1)}, f32[1,256]{1,0:T(1,128)S(1)}, u32[]{:S(2)}, u32[]{:S(2)}) collective-permute-start(f32[1,256]{1,0:T(1,128)S(1)} %add.18), channel_id=1, source_target_pairs={{0,8},{1,9},{2,10},{3,11},{4,12},{5,13},{6,14},{7,15},{8,0},{9,1},... | collective-permute-start | bytes 3080 | tf_op jit(solution)/shard_map/ppermute | solution.py:129
  66.0 3.1 %collective-permute-done.14 = f32[1,256]{1,0:T(1,128)S(1)} collective-permute-done((f32[1,256]{1,0:T(1,128)S(1)}, f32[1,256]{1,0:T(1,128)S(1)}, u32[]{:S(2)}, u32[]{:S(2)}) %collective-permute-start.14) | collective-permute-done | bytes 1056 | tf_op jit(solution)/shard_map/ppermute | solution.py:129
  69.0 0.6 add.19
  (3 shorter events, 0.0 us)
Async XLA Ops:
  0.0 21.9 %collective-permute-start = (bf16[16,8192]{1,0:T(8,128)(2,1)}, bf16[16,8192]{1,0:T(8,128)(2,1)S(1)}, u32[]{:S(2)}, u32[]{:S(2)}) collective-permute-start(bf16[16,8192]{1,0:T(8,128)(2,1)} %refs_0_.1), channel_id=1, source_target_pairs={{0,4},{1,3},{4,8},{5,1},{8,12},{9,5},{12,14},{13,9},{14,10},{15,13... | collective-permute-start | bytes 786440 | tf_op jit(solution)/shard_map/ppermute | solution.py:129
  3.0 26.4 %collective-permute-start.8 = (bf16[16,8192]{1,0:T(8,128)(2,1)}, bf16[16,8192]{1,0:T(8,128)(2,1)S(1)}, u32[]{:S(2)}, u32[]{:S(2)}) collective-permute-start(bf16[16,8192]{1,0:T(8,128)(2,1)} %refs_0_.1), channel_id=1, source_target_pairs={{1,4},{0,3},{5,8},{4,1},{9,12},{8,5},{13,14},{12,9},{15,10},{14,13... | collective-permute-start | bytes 786440 | tf_op jit(solution)/shard_map/ppermute | solution.py:129
  4.4 9.4 %copy-start = (bf16[8192,1792]{1,0:T(8,128)(2,1)S(1)}, bf16[8192,1792]{1,0:T(8,128)(2,1)}, u32[]{:S(2)}) copy-start(bf16[8192,1792]{1,0:T(8,128)(2,1)} %q_ref.7) | copy-start | bytes 88080384
  13.7 1.2 %copy-start.1 = (bf16[256,1792]{1,0:T(8,128)(2,1)S(1)}, bf16[256,1792]{1,0:T(8,128)(2,1)}, u32[]{:S(2)}) copy-start(bf16[256,1792]{1,0:T(8,128)(2,1)} %x_ref.7) | copy-start | bytes 2752516
  17.8 32.8 %collective-permute-start.4 = (f32[128,2048]{1,0:T(8,128)S(1)}, f32[128,2048]{1,0:T(8,128)S(1)}, u32[]{:S(2)}, u32[]{:S(2)}) collective-permute-start(f32[128,2048]{1,0:T(8,128)S(1)} %get-tuple-element.17), channel_id=1, source_target_pairs={{0,1},{1,0},{4,5},{5,4},{8,9},{9,8},{12,13},{13,12},{14,15},{15,14... | collective-permute-start | bytes 3145736 | tf_op jit(solution)/shard_map/ppermute | solution.py:129
  21.8 28.8 %copy-start.2 = (bf16[16,8192]{1,0:T(8,128)(2,1)S(1)}, bf16[16,8192]{1,0:T(8,128)(2,1)}, u32[]{:S(2)}) copy-start(bf16[16,8192]{1,0:T(8,128)(2,1)} %refs_0_.1) | copy-start | bytes 786436
  21.8 28.8 %collective-permute-start.5 = (f32[128,2048]{1,0:T(8,128)S(1)}, f32[128,2048]{1,0:T(8,128)S(1)}, u32[]{:S(2)}, u32[]{:S(2)}) collective-permute-start(f32[128,2048]{1,0:T(8,128)S(1)} %get-tuple-element.18), channel_id=1, source_target_pairs={{0,1},{1,0},{4,5},{5,4},{8,9},{9,8},{12,13},{13,12},{14,15},{15,14... | collective-permute-start | bytes 3145736 | tf_op jit(solution)/shard_map/ppermute | solution.py:129
  21.9 8.1 %collective-permute-start.1 = (bf16[16,8192]{1,0:T(8,128)(2,1)S(1)}, bf16[16,8192]{1,0:T(8,128)(2,1)S(1)}, u32[]{:S(2)}, u32[]{:S(2)}) collective-permute-start(bf16[16,8192]{1,0:T(8,128)(2,1)S(1)} %collective-permute-done.refs_1_), channel_id=1, source_target_pairs={{0,4},{1,3},{4,8},{5,1},{8,12},{9,5},{12,14},{13,9},{14,10},{15,13... | collective-permute-start | bytes 786440 | tf_op jit(solution)/shard_map/ppermute | solution.py:129
  26.4 24.2 %collective-permute-start.6 = (f32[128,2048]{1,0:T(8,128)S(1)}, f32[128,2048]{1,0:T(8,128)S(1)}, u32[]{:S(2)}, u32[]{:S(2)}) collective-permute-start(f32[128,2048]{1,0:T(8,128)S(1)} %get-tuple-element.19), channel_id=1, source_target_pairs={{0,1},{1,0},{4,5},{5,4},{8,9},{9,8},{12,13},{13,12},{14,15},{15,14... | collective-permute-start | bytes 3145736 | tf_op jit(solution)/shard_map/ppermute | solution.py:129
  29.4 21.2 %collective-permute-start.7 = (f32[128,2048]{1,0:T(8,128)S(1)}, f32[128,2048]{1,0:T(8,128)S(1)}, u32[]{:S(2)}, u32[]{:S(2)}) collective-permute-start(f32[128,2048]{1,0:T(8,128)S(1)} %get-tuple-element.20), channel_id=1, source_target_pairs={{0,1},{1,0},{4,5},{5,4},{8,9},{9,8},{12,13},{13,12},{14,15},{15,14... | collective-permute-start | bytes 3145736 | tf_op jit(solution)/shard_map/ppermute | solution.py:129
  30.0 6.4 %collective-permute-start.9 = (bf16[16,8192]{1,0:T(8,128)(2,1)S(1)}, bf16[16,8192]{1,0:T(8,128)(2,1)S(1)}, u32[]{:S(2)}, u32[]{:S(2)}) collective-permute-start(bf16[16,8192]{1,0:T(8,128)(2,1)S(1)} %collective-permute-done.8.refs_2_), channel_id=1, source_target_pairs={{0,4},{1,3},{4,8},{5,1},{8,12},{9,5},{12,14},{13,9},{14,10},{15,13... | collective-permute-start | bytes 786440 | tf_op jit(solution)/shard_map/ppermute | solution.py:129
  36.4 6.4 %collective-permute-start.2 = (bf16[16,8192]{1,0:T(8,128)(2,1)S(1)}, bf16[16,8192]{1,0:T(8,128)(2,1)S(1)}, u32[]{:S(2)}, u32[]{:S(2)}) collective-permute-start(bf16[16,8192]{1,0:T(8,128)(2,1)S(1)} %collective-permute-done.1.refs_3_), channel_id=1, source_target_pairs={{0,4},{1,3},{4,8},{5,1},{8,12},{9,5},{12,14},{13,9},{14,10},{15,13... | collective-permute-start | bytes 786440 | tf_op jit(solution)/shard_map/ppermute | solution.py:129
  42.7 6.4 %collective-permute-start.10 = (bf16[16,8192]{1,0:T(8,128)(2,1)S(1)}, bf16[16,8192]{1,0:T(8,128)(2,1)S(1)}, u32[]{:S(2)}, u32[]{:S(2)}) collective-permute-start(bf16[16,8192]{1,0:T(8,128)(2,1)S(1)} %collective-permute-done.9.refs_4_), channel_id=1, source_target_pairs={{0,4},{1,3},{4,8},{5,1},{8,12},{9,5},{12,14},{13,9},{14,10},{15,13... | collective-permute-start | bytes 786440 | tf_op jit(solution)/shard_map/ppermute | solution.py:129
  49.1 6.4 %collective-permute-start.3 = (bf16[16,8192]{1,0:T(8,128)(2,1)S(1)}, bf16[16,8192]{1,0:T(8,128)(2,1)S(1)}, u32[]{:S(2)}, u32[]{:S(2)}) collective-permute-start(bf16[16,8192]{1,0:T(8,128)(2,1)S(1)} %collective-permute-done.2.refs_5_), channel_id=1, source_target_pairs={{0,4},{1,3},{4,8},{5,1},{8,12},{9,5},{12,14},{13,9},{14,10},{15,13... | collective-permute-start | bytes 786440 | tf_op jit(solution)/shard_map/ppermute | solution.py:129
  56.2 1.2 %collective-permute-start.11 = (f32[1,256]{1,0:T(1,128)S(1)}, f32[1,256]{1,0:T(1,128)S(1)}, u32[]{:S(2)}, u32[]{:S(2)}) collective-permute-start(f32[1,256]{1,0:T(1,128)S(1)} %shard_map.51), channel_id=1, source_target_pairs={{0,1},{1,0},{2,3},{3,2},{4,5},{5,4},{6,7},{7,6},{8,9},{9,8},{10,11... | collective-permute-start | bytes 3080 | tf_op jit(solution)/shard_map/ppermute | solution.py:129
  57.4 3.6 %collective-permute-start.12 = (f32[1,256]{1,0:T(1,128)S(1)}, f32[1,256]{1,0:T(1,128)S(1)}, u32[]{:S(2)}, u32[]{:S(2)}) collective-permute-start(f32[1,256]{1,0:T(1,128)S(1)} %add.16), channel_id=1, source_target_pairs={{0,2},{1,3},{2,0},{3,1},{4,6},{5,7},{6,4},{7,5},{8,10},{9,11},{10,... | collective-permute-start | bytes 3080 | tf_op jit(solution)/shard_map/ppermute | solution.py:129
  61.0 3.6 %collective-permute-start.13 = (f32[1,256]{1,0:T(1,128)S(1)}, f32[1,256]{1,0:T(1,128)S(1)}, u32[]{:S(2)}, u32[]{:S(2)}) collective-permute-start(f32[1,256]{1,0:T(1,128)S(1)} %add.17), channel_id=1, source_target_pairs={{0,4},{1,5},{2,6},{3,7},{4,0},{5,1},{6,2},{7,3},{8,12},{9,13},{10,... | collective-permute-start | bytes 3080 | tf_op jit(solution)/shard_map/ppermute | solution.py:129
  64.6 4.5 %collective-permute-start.14 = (f32[1,256]{1,0:T(1,128)S(1)}, f32[1,256]{1,0:T(1,128)S(1)}, u32[]{:S(2)}, u32[]{:S(2)}) collective-permute-start(f32[1,256]{1,0:T(1,128)S(1)} %add.18), channel_id=1, source_target_pairs={{0,8},{1,9},{2,10},{3,11},{4,12},{5,13},{6,14},{7,15},{8,0},{9,1},... | collective-permute-start | bytes 3080 | tf_op jit(solution)/shard_map/ppermute | solution.py:129

commit v2 on v0

v2 whole, which is shorter than its diff:
```python
import functools

import jax
import jax.numpy as jnp
import numpy as np
from jax import lax
from jax.experimental import pallas as pl
from jax.experimental.pallas import tpu as pltpu
from jax.sharding import PartitionSpec as P

SPLIT = (2048, 2048, 2048, 2048)
STEP = 512
LANES = 128
SLOTS = 3
GROUP = 14
GRANT = 10 << 20
VMEM = pl.BlockSpec(memory_space=pltpu.VMEM)
SMEM = pl.BlockSpec(memory_space=pltpu.SMEM)
HBM = pl.BlockSpec(memory_space=pltpu.HBM)
ANY = pl.BlockSpec(memory_space=pl.ANY)


def ring_of(units):
    chips = units // 2
    if units != 16:
        return [2 * chip for chip in range(chips)]
    there = [2 * chip for chip in range(0, chips, 2)]
    return there + [2 * chip for chip in range(chips - 1, 0, -2)]


def plan(units):
    ring = ring_of(units)
    chips = len(ring)
    at = lambda place, core: ring[place % chips] + core
    ahead, across, twin = [], [], []
    held = np.zeros((units, chips), np.int32)
    for place in range(chips):
        for core, way in ((0, 1), (1, -1)):
            me = at(place, core)
            ahead.append((me, at(place + way, core)))
            across.append((at(place, 1 - core), at(place + way, core)))
            twin.append((me, at(place, 1 - core)))
            blocks = [me]
            for hop in range(1, chips // 2):
                blocks += [at(place - way * hop, core), at(place - way * hop, 1 - core)]
            blocks.append(at(place - way * (chips // 2), core))
            held[me] = blocks
    other = np.array([dict(twin)[unit] for unit in range(units)])
    return ahead, across, twin, np.concatenate([held, held[other]], axis=1)


def weigh_kernel(first, width, following, waits, order, x_ref, q_ref, *refs):
    steps = width // STEP
    begin = first == 0
    refs = list(refs)
    slab = None if begin else refs.pop(0)
    del refs[:waits]
    weights_ref = refs[1 if begin else 0]
    next_slab = refs[2 if begin else 1] if following else None

    def at(i):
        return pl.ds(pl.multiple_of(i * STEP, STEP), STEP)

    def fetch(start, i, to, sem, slots):
        here = pl.ds(pl.multiple_of(start + i * STEP, STEP), STEP)
        slot = lax.rem(i, slots)
        return pltpu.make_async_copy(q_ref.at[here], to.at[at(slot)], sem.at[slot])

    if begin:
        x, own, placed, ready, coming = refs[0], *refs[-4:]
        copy = pltpu.make_async_copy(x_ref, x, placed)
        copy.start()
        for i in range(SLOTS):
            fetch(first, i, own, ready, SLOTS).start()
        copy.wait()
    else:
        x, own, coming = x_ref, slab, refs[-1]
        for i in range(following // STEP):
            fetch(first + width, i, next_slab, coming, steps).start()

    @pl.loop(0, steps)
    def _(i):
        if begin:
            fetch(first, i, own, ready, SLOTS).wait()
        weights_ref[:, at(i)] = lax.dot_general(
            x[...],
            own[at(lax.rem(i, SLOTS) if begin else i), :],
            (((1,), (1,)), ((), ())),
            preferred_element_type=jnp.float32,
        )
        if begin:

            @pl.when(i + SLOTS < steps)
            def _():
                fetch(first, i + SLOTS, own, ready, SLOTS).start()

            @pl.when(i < following // STEP)
            def _():
                fetch(first + width, i, next_slab, coming, steps).start()

    for i in range(following // STEP):
        fetch(first + width, i, next_slab, coming, steps).wait()


def weigh(first, width, following, order, x, q, slab, after):
    tokens, depth = x.shape
    begin = first == 0
    out_shape, scratch = [], []
    if begin:
        out_shape.append(pltpu.VMEM(x.shape, x.dtype))
        scratch = [
            pltpu.VMEM((SLOTS * STEP, depth), q.dtype),
            pltpu.SemaphoreType.DMA,
            pltpu.SemaphoreType.DMA((SLOTS,)),
        ]
    out_shape.append(pltpu.VMEM((tokens, width), jnp.float32))
    if following:
        out_shape.append(pltpu.VMEM((following, depth), q.dtype))
    return pl.pallas_call(
        functools.partial(weigh_kernel, first, width, following, len(after)),
        in_specs=[SMEM] + ([HBM, HBM] if begin else [VMEM, HBM, VMEM] + [ANY] * len(after)),
        out_specs=[VMEM] * len(out_shape),
        out_shape=out_shape,
        scratch_shapes=scratch + [pltpu.SemaphoreType.DMA((max(following, STEP) // STEP,))],
        compiler_params=pltpu.CompilerParams(vmem_limit_bytes=GRANT),
        cost_estimate=pl.CostEstimate(
            flops=2 * tokens * depth * width,
            bytes_accessed=2 * depth * width,
            transcendentals=0,
        ),
    )(order, x, q, *([] if begin else [slab, *after]))


def dots(gradient, start, weights):
    block = gradient.shape[0]
    total = jnp.zeros((block, LANES), jnp.float32)
    at = 0
    for piece in weights:
        for lane in range(0, piece.shape[1], LANES):
            weight = piece[pl.ds(start, block), lane : lane + LANES]
            total += gradient[:, at : at + LANES].astype(jnp.float32) * weight
            at += LANES
    return total


def table_kernel(places, finish, order, *refs):
    count = len(places)
    gradients, weights = refs[:count], refs[count : count + len(SPLIT)]
    more = refs[count + len(SPLIT) :]
    out = more[-1]
    table = more[-1]
    if finish:
        out, table = more[-2:]
    if len(more) > 1 + finish:
        table[...] = more[0][...]
    else:
        table[...] = jnp.zeros_like(table)
    block = gradients[0].shape[0]
    for place, gradient in zip(places, gradients):
        start = pl.multiple_of(order[place] * block, block)
        table[pl.ds(start, block), :] = dots(gradient, start, weights)
    if finish:
        out[...] = jnp.sum(table[...].T, axis=0, keepdims=True)


def add_blocks(places, order, gradients, weights, table, finish):
    tokens = weights[0].shape[0]
    shape = (tokens, LANES)
    extra = [] if table is None else [table]
    return pl.pallas_call(
        functools.partial(table_kernel, places, finish),
        in_specs=[SMEM] + [VMEM] * (len(gradients) + len(weights) + len(extra)),
        out_specs=VMEM,
        out_shape=jax.ShapeDtypeStruct((1, tokens) if finish else shape, jnp.float32),
        scratch_shapes=[pltpu.VMEM(shape, jnp.float32)] * finish,
        compiler_params=pltpu.CompilerParams(vmem_limit_bytes=GRANT),
    )(order, *gradients, *weights, *extra)


def in_vmem(arrays):
    return [pltpu.with_memory_space_constraint(array, pltpu.VMEM) for array in arrays]


def body(units, query_grad, out_grads, inputs):
    ahead, across, twin, orders = plan(units)
    send = lambda value, pairs: lax.ppermute(value, "unit", pairs)
    order = jnp.asarray(orders)[lax.axis_index("unit")]
    tokens = inputs.shape[0]
    half = units // 2

    weights, slabs, rows = [], [], []
    resident = pltpu.with_memory_space_constraint(query_grad, pltpu.HBM)

    def piece(*after):
        done = len(weights)
        following = SPLIT[done + 1] if done + 1 < len(SPLIT) else 0
        x = rows[0] if done else pltpu.with_memory_space_constraint(inputs, pltpu.HBM)
        made = list(weigh(
            sum(SPLIT[:done]), SPLIT[done], following, order, x, resident, slabs[-1] if done else None, after
        ))
        if not done:
            rows.extend(in_vmem([made.pop(0)]))
        weights.extend(in_vmem([made.pop(0)]))
        slabs.extend(in_vmem(made))

    def later(value):
        return lax.optimization_barrier((value, weights[-1]))[0]

    hops = units // 4
    held = [out_grads, send(out_grads, ahead), send(out_grads, across)]
    piece()
    for hop in range(1, hops):
        same, other = held[-2:]
        held.append(send(later(same), ahead))
        if hop + 1 == hops:
            break
        if hop > 1 and len(weights) < len(SPLIT):
            piece(same)
        held.append(send(later(other) if hop > 1 else other, ahead))
        if len(weights) < len(SPLIT):
            piece(*([same, other] if hop == 1 else [other]))
    blocks = held + [send(value, twin) for value in held]

    final = [half - 1, units - 1]
    rest = [place for place in range(units) if place not in final]
    table = None
    for group in range(0, len(rest), GROUP):
        places = rest[group : group + GROUP]
        table = add_blocks(places, order, [blocks[place] for place in places], weights, table, False)
    partial_value = add_blocks(final, order, [blocks[place] for place in final], weights, table, True)

    bit = 1
    while bit < units:
        pairs = [(unit, unit ^ bit) for unit in range(units)]
        partial_value += send(partial_value, pairs)
        bit *= 2
    return partial_value.reshape(tokens)


def solution(mesh):
    return jax.shard_map(
        functools.partial(body, mesh.shape["unit"]),
        mesh=mesh,
        in_specs=(P("job", "unit"), P(("job", "unit"), None), P("job", "unit")),
        out_specs=P("job"),
        check_vma=False,
    )
```

time: 117 us -> 51.2 us (0.44)
  waiting for transfers between devices: 56.3 us -> 15.6 us
  blocking collectives: 31.7 us -> 0 us
  Pallas kernels: 0 us -> 20 us
  matrix products: 15 us -> 0 us
  starting transfers between devices: 0.01 us -> 14.1 us
  between operations: 13.4 us -> 0.11 us
    all_gather x1 -> x0, waiting for transfers between devices: 55.6 us -> none  [body(): lax.all_gather(out_grads, 'unit', axis=0, tiled=True)]
    psum x1 -> x0, blocking collectives: 31.7 us -> none  [body(): return lax.psum(partial_value, 'unit')]
    pallas_call x0 -> x6, Pallas kernels: none -> 20 us  [the longest x4 17.9 us: weigh(): pl.pallas_call(functools.partial(weigh_kernel, first, width, following, l...]
    ppermute x0 -> x19, waiting for transfers between devices: none -> 15.6 us  [body(): send = lambda value, pairs: lax.ppermute(value, 'unit', pairs)]
    dot_general x1 -> x0, matrix products: 15 us -> none  [body(): jnp.dot(lax.all_gather(out_grads, 'unit', axis=0, tiled=True), query_grad...]
    ppermute x0 -> x19, starting transfers between devices: none -> 14.1 us  [body(): send = lambda value, pairs: lax.ppermute(value, 'unit', pairs)]
  transfers between devices with their start and end apart: 1 -> 19, of which waited for: 1 -> 7; matrix products, arithmetic and copies ran while one was open for 0% -> 1% of each run, Pallas kernels for 0% -> 38%
where the time goes in v2:
time: 51.2 us; the launch traced here: 51.1 us
  Pallas kernels  20 us (39%)
  waiting for transfers between devices  15.6 us (30%)
  starting transfers between devices  14.1 us (28%)
  local copies, waits for them, and re-layouts  0.69 us (1%)
  other arithmetic  0.57 us (1%)
    pallas_call x4, Pallas kernels, weigh(): pl.pallas_call(functools.partial(weigh_kernel, first, width, following, l...  17.9 us
    ppermute x19, waiting for transfers between devices, body(): send = lambda value, pairs: lax.ppermute(value, 'unit', pairs)  15.6 us
    ppermute x19, starting transfers between devices, body(): send = lambda value, pairs: lax.ppermute(value, 'unit', pairs)  14.1 us
    pallas_call x2, Pallas kernels, add_blocks(): pl.pallas_call(functools.partial(table_kernel, places, finish), in_specs=...  2.14 us
  transfers between devices with their start and end apart: 19, of which 7 were waited for; matrix products, arithmetic and copies ran while one was open for 1% of the time, Pallas kernels for 38%

profile of v2, /device:TPU:0, one launch (start us, length us, event | category | flops | bytes accessed | tf_op | source)
XLA Modules:
  0.0 51.1 jit_solution(9660720239467075800)
XLA Ops:
  0.0 3.0 %collective-permute-start = (bf16[16,8192]{1,0:T(8,128)(2,1)}, bf16[16,8192]{1,0:T(8,128)(2,1)S(1)}, u32[]{:S(2)}, u32[]{:S(2)}) collective-permute-start(bf16[16,8192]{1,0:T(8,128)(2,1)} %refs_0_.1), channel_id=1, source_target_pairs={{0,4},{1,3},{4,8},{5,1},{8,12},{9,5},{12,14},{13,9},{14,10},{15,13... | collective-permute-start | bytes 786440 | tf_op jit(solution)/shard_map/ppermute | solution.py:186
  3.0 0.7 %collective-permute-start.2 = (bf16[16,8192]{1,0:T(8,128)(2,1)}, bf16[16,8192]{1,0:T(8,128)(2,1)S(1)}, u32[]{:S(2)}, u32[]{:S(2)}) collective-permute-start(bf16[16,8192]{1,0:T(8,128)(2,1)} %refs_0_.1), channel_id=1, source_target_pairs={{1,4},{0,3},{5,8},{4,1},{9,12},{8,5},{13,14},{12,9},{15,10},{14,13... | collective-permute-start | bytes 786440 | tf_op jit(solution)/shard_map/ppermute | solution.py:186
  3.7 0.7 %dynamic-slice_bitcast_fusion.order = s32[16]{0:T(128)S(1)} fusion(s32[16,16]{1,0:T(8,128)} %constant.10.clone, s32[]{:T(128)S(6)} %select_n.3), kind=kLoop, calls=%fused_computation | loop fusion | bytes 132 | tf_op jit(solution)/shard_map/squeeze | solution.py:187
  4.4 0.0 copy-start
  4.4 7.2 %shard_map.46 = (bf16[256,1792]{1,0:T(8,128)(2,1)S(1)}, f32[256,2048]{1,0:T(8,128)S(1)}, bf16[2048,1792]{1,0:T(8,128)(2,1)S(1)}) custom-call(s32[16]{0:T(128)S(1)} %dynamic-slice_bitcast_fusion.order, bf16[256,1792]{1,0:T(8,128)(2,1)} %x_ref.1, bf16[8192,1792]{1,0:T(8,128)(2,1)} %q_ref.7), custom_call_target="tpu_custom_call" | custom-call | flops 1879048192 | bytes 7340032 | tf_op jit(solution)/shard_map/pallas_call | solution.py:119
  11.6 0.0 collective-permute-done.refs_1_
  11.6 0.9 %collective-permute-start.1 = (bf16[16,8192]{1,0:T(8,128)(2,1)S(1)}, bf16[16,8192]{1,0:T(8,128)(2,1)S(1)}, u32[]{:S(2)}, u32[]{:S(2)}) collective-permute-start(bf16[16,8192]{1,0:T(8,128)(2,1)S(1)} %collective-permute-done.refs_1_), channel_id=1, source_target_pairs={{0,4},{1,3},{4,8},{5,1},{8,12},{9,5},{12,14},{13,9},{14,10},{15,13... | collective-permute-start | bytes 786440 | tf_op jit(solution)/shard_map/ppermute | solution.py:186
  12.6 0.0 copy-done
  12.6 0.3 collective-permute-start.8
  12.8 0.0 collective-permute-done.2.refs_2_
  12.8 1.6 %collective-permute-start.4 = (bf16[16,8192]{1,0:T(8,128)(2,1)S(1)}, bf16[16,8192]{1,0:T(8,128)(2,1)S(1)}, u32[]{:S(2)}, u32[]{:S(2)}) collective-permute-start(bf16[16,8192]{1,0:T(8,128)(2,1)S(1)} %collective-permute-done.2.refs_2_), channel_id=1, source_target_pairs={{0,4},{1,3},{4,8},{5,1},{8,12},{9,5},{12,14},{13,9},{14,10},{15,13... | collective-permute-start | bytes 786440 | tf_op jit(solution)/shard_map/ppermute | solution.py:186
  14.4 0.0 collective-permute-start.10
  14.4 0.5 collective-permute-start.9
  14.9 3.7 %shard_map.47 = (f32[256,2048]{1,0:T(8,128)S(1)}, bf16[2048,1792]{1,0:T(8,128)(2,1)S(1)}) custom-call(s32[16]{0:T(128)S(1)} %dynamic-slice_bitcast_fusion.order, bf16[256,1792]{1,0:T(8,128)(2,1)S(1)} %get-tuple-element.18.x_ref, bf16[8192,1792]{1,0:T(8,128)(2,1)} %q_ref.7, bf16[2048,1792]{1,0:T(8,128)(2,1)S(1)} %get-tuple-element.19.refs_0_, ...), custom_call_target="tpu_custom_call" | custom-call | flops 1879048192 | bytes 7340032 | tf_op jit(solution)/shard_map/pallas_call | solution.py:119
  18.7 0.0 collective-permute-done.1.refs_1_.refs_3_
  18.7 1.6 %collective-permute-start.3 = (bf16[16,8192]{1,0:T(8,128)(2,1)S(1)}, bf16[16,8192]{1,0:T(8,128)(2,1)S(1)}, u32[]{:S(2)}, u32[]{:S(2)}) collective-permute-start(bf16[16,8192]{1,0:T(8,128)(2,1)S(1)} %collective-permute-done.1.refs_1_.refs_3_), channel_id=1, source_target_pairs={{0,4},{1,3},{4,8},{5,1},{8,12},{9,5},{12,14},{13,9},{14,10},{15,13... | collective-permute-start | bytes 786440 | tf_op jit(solution)/shard_map/ppermute | solution.py:186
  20.3 3.7 %shard_map.48 = (f32[256,2048]{1,0:T(8,128)S(1)}, bf16[2048,1792]{1,0:T(8,128)(2,1)S(1)}) custom-call(s32[16]{0:T(128)S(1)} %dynamic-slice_bitcast_fusion.order, bf16[256,1792]{1,0:T(8,128)(2,1)S(1)} %get-tuple-element.18.x_ref, bf16[8192,1792]{1,0:T(8,128)(2,1)} %q_ref.7, bf16[2048,1792]{1,0:T(8,128)(2,1)S(1)} %get-tuple-element.22.refs_0_, ...), custom_call_target="tpu_custom_call" | custom-call | flops 1879048192 | bytes 7340032 | tf_op jit(solution)/shard_map/pallas_call | solution.py:119
  24.0 0.0 collective-permute-done.4.refs_1_.refs_4_
  24.0 1.6 %collective-permute-start.7 = (bf16[16,8192]{1,0:T(8,128)(2,1)S(1)}, bf16[16,8192]{1,0:T(8,128)(2,1)S(1)}, u32[]{:S(2)}, u32[]{:S(2)}) collective-permute-start(bf16[16,8192]{1,0:T(8,128)(2,1)S(1)} %collective-permute-done.4.refs_1_.refs_4_), channel_id=1, source_target_pairs={{0,4},{1,3},{4,8},{5,1},{8,12},{9,5},{12,14},{13,9},{14,10},{15,13... | collective-permute-start | bytes 786440 | tf_op jit(solution)/shard_map/ppermute | solution.py:186
  25.6 3.2 %shard_map.49.refs_17_.refs_5_ = f32[256,2048]{1,0:T(8,128)S(1)} custom-call(s32[16]{0:T(128)S(1)} %dynamic-slice_bitcast_fusion.order, bf16[256,1792]{1,0:T(8,128)(2,1)S(1)} %get-tuple-element.18.x_ref, bf16[8192,1792]{1,0:T(8,128)(2,1)} %q_ref.7, bf16[2048,1792]{1,0:T(8,128)(2,1)S(1)} %get-tuple-element.23.refs_0_, ...), custom_call_target="tpu_custom_call" | custom-call | flops 1879048192 | bytes 7340032 | tf_op jit(solution)/shard_map/pallas_call | solution.py:119
  28.9 0.0 collective-permute-done.3.refs_5_
  28.9 0.5 collective-permute-start.5
  29.4 0.0 collective-permute-done.8.refs_7_
  29.4 0.0 collective-permute-start.11
  29.4 0.0 collective-permute-done.10.refs_9_
  29.4 0.5 collective-permute-start.12
  29.9 0.6 %collective-permute-done.7.refs_6_ = bf16[16,8192]{1,0:T(8,128)(2,1)S(1)} collective-permute-done((bf16[16,8192]{1,0:T(8,128)(2,1)S(1)}, bf16[16,8192]{1,0:T(8,128)(2,1)S(1)}, u32[]{:S(2)}, u32[]{:S(2)}) %collective-permute-start.7) | collective-permute-done | bytes 262176 | tf_op jit(solution)/shard_map/ppermute | solution.py:186
  30.5 0.0 collective-permute-start.14
  30.5 0.0 collective-permute-done.9.refs_8_
  30.5 0.5 collective-permute-start.13
  31.0 4.3 %collective-permute-done.5.refs_0_ = bf16[16,8192]{1,0:T(8,128)(2,1)S(1)} collective-permute-done((bf16[16,8192]{1,0:T(8,128)(2,1)S(1)}, bf16[16,8192]{1,0:T(8,128)(2,1)S(1)}, u32[]{:S(2)}, u32[]{:S(2)}) %collective-permute-start.5) | collective-permute-done | bytes 262176 | tf_op jit(solution)/shard_map/ppermute | solution.py:186
  35.3 0.0 collective-permute-start.6
  35.3 0.0 collective-permute-done.11.refs_10_
  35.3 0.0 collective-permute-done.12.refs_11_
  35.3 0.0 collective-permute-done.14.refs_13_
  35.3 0.0 collective-permute-done.13.refs_12_
  35.3 1.4 %shard_map.50.refs_6_ = f32[256,128]{1,0:T(8,128)S(1)} custom-call(s32[16]{0:T(128)S(1)} %dynamic-slice_bitcast_fusion.order, bf16[16,8192]{1,0:T(8,128)(2,1)S(1)} %copy-done, bf16[16,8192]{1,0:T(8,128)(2,1)S(1)} %collective-permute-done.refs_1_, bf16[16,8192]{1,0:T(8,128)(2,1)S(1)} %collective-permute-done.2.refs_2_, ...), custom_call_target="tpu_custom_call" | custom-call | tf_op jit(solution)/shard_map/pallas_call | solution.py:170
  36.7 0.1 collective-permute-done.6.refs_1_
  36.8 0.8 %shard_map.51 = f32[1,256]{1,0:T(1,128)S(1)} custom-call(s32[16]{0:T(128)S(1)} %dynamic-slice_bitcast_fusion.order, bf16[16,8192]{1,0:T(8,128)(2,1)S(1)} %collective-permute-done.5.refs_0_, bf16[16,8192]{1,0:T(8,128)(2,1)S(1)} %collective-permute-done.6.refs_1_, f32[256,2048]{1,0:T(8,128)S(1)} %get-tuple-element.16.refs_14_.refs_2_, ...), custom_call_target="tpu_custom_call" | custom-call | tf_op jit(solution)/shard_map/pallas_call | solution.py:170
  37.6 0.4 collective-permute-start.15
  38.0 0.8 %collective-permute-done.15 = f32[1,256]{1,0:T(1,128)S(1)} collective-permute-done((f32[1,256]{1,0:T(1,128)S(1)}, f32[1,256]{1,0:T(1,128)S(1)}, u32[]{:S(2)}, u32[]{:S(2)}) %collective-permute-start.15) | collective-permute-done | bytes 1056 | tf_op jit(solution)/shard_map/ppermute | solution.py:186
  38.9 0.5 collective-permute-start.16
  39.4 3.1 %collective-permute-done.16 = f32[1,256]{1,0:T(1,128)S(1)} collective-permute-done((f32[1,256]{1,0:T(1,128)S(1)}, f32[1,256]{1,0:T(1,128)S(1)}, u32[]{:S(2)}, u32[]{:S(2)}) %collective-permute-start.16) | collective-permute-done | bytes 1056 | tf_op jit(solution)/shard_map/ppermute | solution.py:186
  42.4 0.5 collective-permute-start.17
  42.9 3.1 %collective-permute-done.17 = f32[1,256]{1,0:T(1,128)S(1)} collective-permute-done((f32[1,256]{1,0:T(1,128)S(1)}, f32[1,256]{1,0:T(1,128)S(1)}, u32[]{:S(2)}, u32[]{:S(2)}) %collective-permute-start.17) | collective-permute-done | bytes 1056 | tf_op jit(solution)/shard_map/ppermute | solution.py:186
  46.0 1.0 %collective-permute-start.18 = (f32[1,256]{1,0:T(1,128)S(1)}, f32[1,256]{1,0:T(1,128)S(1)}, u32[]{:S(2)}, u32[]{:S(2)}) collective-permute-start(f32[1,256]{1,0:T(1,128)S(1)} %add.18), channel_id=1, source_target_pairs={{0,8},{1,9},{2,10},{3,11},{4,12},{5,13},{6,14},{7,15},{8,0},{9,1},... | collective-permute-start | bytes 3080 | tf_op jit(solution)/shard_map/ppermute | solution.py:186
  47.0 3.5 %collective-permute-done.18 = f32[1,256]{1,0:T(1,128)S(1)} collective-permute-done((f32[1,256]{1,0:T(1,128)S(1)}, f32[1,256]{1,0:T(1,128)S(1)}, u32[]{:S(2)}, u32[]{:S(2)}) %collective-permute-start.18) | collective-permute-done | bytes 1056 | tf_op jit(solution)/shard_map/ppermute | solution.py:186
  50.5 0.6 %add.19 = f32[1,256]{1,0:T(1,128)} add(f32[1,256]{1,0:T(1,128)S(1)} %add.18, f32[1,256]{1,0:T(1,128)S(1)} %collective-permute-done.18) | non-fusion elementwise | flops 256 | bytes 3072 | tf_op jit(solution)/shard_map/add | solution.py:235
  (3 shorter events, 0.0 us)
Async XLA Ops:
  0.0 11.6 %collective-permute-start = (bf16[16,8192]{1,0:T(8,128)(2,1)}, bf16[16,8192]{1,0:T(8,128)(2,1)S(1)}, u32[]{:S(2)}, u32[]{:S(2)}) collective-permute-start(bf16[16,8192]{1,0:T(8,128)(2,1)} %refs_0_.1), channel_id=1, source_target_pairs={{0,4},{1,3},{4,8},{5,1},{8,12},{9,5},{12,14},{13,9},{14,10},{15,13... | collective-permute-start | bytes 786440 | tf_op jit(solution)/shard_map/ppermute | solution.py:186
  3.0 9.8 %collective-permute-start.2 = (bf16[16,8192]{1,0:T(8,128)(2,1)}, bf16[16,8192]{1,0:T(8,128)(2,1)S(1)}, u32[]{:S(2)}, u32[]{:S(2)}) collective-permute-start(bf16[16,8192]{1,0:T(8,128)(2,1)} %refs_0_.1), channel_id=1, source_target_pairs={{1,4},{0,3},{5,8},{4,1},{9,12},{8,5},{13,14},{12,9},{15,10},{14,13... | collective-permute-start | bytes 786440 | tf_op jit(solution)/shard_map/ppermute | solution.py:186
  4.4 8.2 %copy-start = (bf16[16,8192]{1,0:T(8,128)(2,1)S(1)}, bf16[16,8192]{1,0:T(8,128)(2,1)}, u32[]{:S(2)}) copy-start(bf16[16,8192]{1,0:T(8,128)(2,1)} %refs_0_.1) | copy-start | bytes 786436
  11.6 7.1 %collective-permute-start.1 = (bf16[16,8192]{1,0:T(8,128)(2,1)S(1)}, bf16[16,8192]{1,0:T(8,128)(2,1)S(1)}, u32[]{:S(2)}, u32[]{:S(2)}) collective-permute-start(bf16[16,8192]{1,0:T(8,128)(2,1)S(1)} %collective-permute-done.refs_1_), channel_id=1, source_target_pairs={{0,4},{1,3},{4,8},{5,1},{8,12},{9,5},{12,14},{13,9},{14,10},{15,13... | collective-permute-start | bytes 786440 | tf_op jit(solution)/shard_map/ppermute | solution.py:186
  12.6 16.8 %collective-permute-start.8 = (bf16[16,8192]{1,0:T(8,128)(2,1)S(1)}, bf16[16,8192]{1,0:T(8,128)(2,1)S(1)}, u32[]{:S(2)}, u32[]{:S(2)}) collective-permute-start(bf16[16,8192]{1,0:T(8,128)(2,1)S(1)} %copy-done), channel_id=1, source_target_pairs={{0,1},{1,0},{4,5},{5,4},{8,9},{9,8},{12,13},{13,12},{14,15},{15,14... | collective-permute-start | bytes 786440 | tf_op jit(solution)/shard_map/ppermute | solution.py:186
  12.8 11.2 %collective-permute-start.4 = (bf16[16,8192]{1,0:T(8,128)(2,1)S(1)}, bf16[16,8192]{1,0:T(8,128)(2,1)S(1)}, u32[]{:S(2)}, u32[]{:S(2)}) collective-permute-start(bf16[16,8192]{1,0:T(8,128)(2,1)S(1)} %collective-permute-done.2.refs_2_), channel_id=1, source_target_pairs={{0,4},{1,3},{4,8},{5,1},{8,12},{9,5},{12,14},{13,9},{14,10},{15,13... | collective-permute-start | bytes 786440 | tf_op jit(solution)/shard_map/ppermute | solution.py:186
  14.4 15.0 %collective-permute-start.10 = (bf16[16,8192]{1,0:T(8,128)(2,1)S(1)}, bf16[16,8192]{1,0:T(8,128)(2,1)S(1)}, u32[]{:S(2)}, u32[]{:S(2)}) collective-permute-start(bf16[16,8192]{1,0:T(8,128)(2,1)S(1)} %collective-permute-done.2.refs_2_), channel_id=1, source_target_pairs={{0,1},{1,0},{4,5},{5,4},{8,9},{9,8},{12,13},{13,12},{14,15},{15,14... | collective-permute-start | bytes 786440 | tf_op jit(solution)/shard_map/ppermute | solution.py:186
  14.4 16.1 %collective-permute-start.9 = (bf16[16,8192]{1,0:T(8,128)(2,1)S(1)}, bf16[16,8192]{1,0:T(8,128)(2,1)S(1)}, u32[]{:S(2)}, u32[]{:S(2)}) collective-permute-start(bf16[16,8192]{1,0:T(8,128)(2,1)S(1)} %collective-permute-done.refs_1_), channel_id=1, source_target_pairs={{0,1},{1,0},{4,5},{5,4},{8,9},{9,8},{12,13},{13,12},{14,15},{15,14... | collective-permute-start | bytes 786440 | tf_op jit(solution)/shard_map/ppermute | solution.py:186
  18.7 10.2 %collective-permute-start.3 = (bf16[16,8192]{1,0:T(8,128)(2,1)S(1)}, bf16[16,8192]{1,0:T(8,128)(2,1)S(1)}, u32[]{:S(2)}, u32[]{:S(2)}) collective-permute-start(bf16[16,8192]{1,0:T(8,128)(2,1)S(1)} %collective-permute-done.1.refs_1_.refs_3_), channel_id=1, source_target_pairs={{0,4},{1,3},{4,8},{5,1},{8,12},{9,5},{12,14},{13,9},{14,10},{15,13... | collective-permute-start | bytes 786440 | tf_op jit(solution)/shard_map/ppermute | solution.py:186
  24.0 6.4 %collective-permute-start.7 = (bf16[16,8192]{1,0:T(8,128)(2,1)S(1)}, bf16[16,8192]{1,0:T(8,128)(2,1)S(1)}, u32[]{:S(2)}, u32[]{:S(2)}) collective-permute-start(bf16[16,8192]{1,0:T(8,128)(2,1)S(1)} %collective-permute-done.4.refs_1_.refs_4_), channel_id=1, source_target_pairs={{0,4},{1,3},{4,8},{5,1},{8,12},{9,5},{12,14},{13,9},{14,10},{15,13... | collective-permute-start | bytes 786440 | tf_op jit(solution)/shard_map/ppermute | solution.py:186
  28.9 6.4 %collective-permute-start.5 = (bf16[16,8192]{1,0:T(8,128)(2,1)S(1)}, bf16[16,8192]{1,0:T(8,128)(2,1)S(1)}, u32[]{:S(2)}, u32[]{:S(2)}) collective-permute-start(bf16[16,8192]{1,0:T(8,128)(2,1)S(1)} %collective-permute-done.3.refs_5_), channel_id=1, source_target_pairs={{0,4},{1,3},{4,8},{5,1},{8,12},{9,5},{12,14},{13,9},{14,10},{15,13... | collective-permute-start | bytes 786440 | tf_op jit(solution)/shard_map/ppermute | solution.py:186
  29.4 5.9 %collective-permute-start.11 = (bf16[16,8192]{1,0:T(8,128)(2,1)S(1)}, bf16[16,8192]{1,0:T(8,128)(2,1)S(1)}, u32[]{:S(2)}, u32[]{:S(2)}) collective-permute-start(bf16[16,8192]{1,0:T(8,128)(2,1)S(1)} %collective-permute-done.1.refs_1_.refs_3_), channel_id=1, source_target_pairs={{0,1},{1,0},{4,5},{5,4},{8,9},{9,8},{12,13},{13,12},{14,15},{15,14... | collective-permute-start | bytes 786440 | tf_op jit(solution)/shard_map/ppermute | solution.py:186
  29.4 5.9 %collective-permute-start.12 = (bf16[16,8192]{1,0:T(8,128)(2,1)S(1)}, bf16[16,8192]{1,0:T(8,128)(2,1)S(1)}, u32[]{:S(2)}, u32[]{:S(2)}) collective-permute-start(bf16[16,8192]{1,0:T(8,128)(2,1)S(1)} %collective-permute-done.4.refs_1_.refs_4_), channel_id=1, source_target_pairs={{0,1},{1,0},{4,5},{5,4},{8,9},{9,8},{12,13},{13,12},{14,15},{15,14... | collective-permute-start | bytes 786440 | tf_op jit(solution)/shard_map/ppermute | solution.py:186
  30.5 4.8 %collective-permute-start.14 = (bf16[16,8192]{1,0:T(8,128)(2,1)S(1)}, bf16[16,8192]{1,0:T(8,128)(2,1)S(1)}, u32[]{:S(2)}, u32[]{:S(2)}) collective-permute-start(bf16[16,8192]{1,0:T(8,128)(2,1)S(1)} %collective-permute-done.7.refs_6_), channel_id=1, source_target_pairs={{0,1},{1,0},{4,5},{5,4},{8,9},{9,8},{12,13},{13,12},{14,15},{15,14... | collective-permute-start | bytes 786440 | tf_op jit(solution)/shard_map/ppermute | solution.py:186
  30.5 4.8 %collective-permute-start.13 = (bf16[16,8192]{1,0:T(8,128)(2,1)S(1)}, bf16[16,8192]{1,0:T(8,128)(2,1)S(1)}, u32[]{:S(2)}, u32[]{:S(2)}) collective-permute-start(bf16[16,8192]{1,0:T(8,128)(2,1)S(1)} %collective-permute-done.3.refs_5_), channel_id=1, source_target_pairs={{0,1},{1,0},{4,5},{5,4},{8,9},{9,8},{12,13},{13,12},{14,15},{15,14... | collective-permute-start | bytes 786440 | tf_op jit(solution)/shard_map/ppermute | solution.py:186
  35.3 1.5 %collective-permute-start.6 = (bf16[16,8192]{1,0:T(8,128)(2,1)S(1)}, bf16[16,8192]{1,0:T(8,128)(2,1)S(1)}, u32[]{:S(2)}, u32[]{:S(2)}) collective-permute-start(bf16[16,8192]{1,0:T(8,128)(2,1)S(1)} %collective-permute-done.5.refs_0_), channel_id=1, source_target_pairs={{0,1},{1,0},{4,5},{5,4},{8,9},{9,8},{12,13},{13,12},{14,15},{15,14... | collective-permute-start | bytes 786440 | tf_op jit(solution)/shard_map/ppermute | solution.py:186
  37.6 1.2 %collective-permute-start.15 = (f32[1,256]{1,0:T(1,128)S(1)}, f32[1,256]{1,0:T(1,128)S(1)}, u32[]{:S(2)}, u32[]{:S(2)}) collective-permute-start(f32[1,256]{1,0:T(1,128)S(1)} %shard_map.51), channel_id=1, source_target_pairs={{0,1},{1,0},{2,3},{3,2},{4,5},{5,4},{6,7},{7,6},{8,9},{9,8},{10,11... | collective-permute-start | bytes 3080 | tf_op jit(solution)/shard_map/ppermute | solution.py:186
  38.9 3.6 %collective-permute-start.16 = (f32[1,256]{1,0:T(1,128)S(1)}, f32[1,256]{1,0:T(1,128)S(1)}, u32[]{:S(2)}, u32[]{:S(2)}) collective-permute-start(f32[1,256]{1,0:T(1,128)S(1)} %add.16), channel_id=1, source_target_pairs={{0,2},{1,3},{2,0},{3,1},{4,6},{5,7},{6,4},{7,5},{8,10},{9,11},{10,... | collective-permute-start | bytes 3080 | tf_op jit(solution)/shard_map/ppermute | solution.py:186
  42.4 3.6 %collective-permute-start.17 = (f32[1,256]{1,0:T(1,128)S(1)}, f32[1,256]{1,0:T(1,128)S(1)}, u32[]{:S(2)}, u32[]{:S(2)}) collective-permute-start(f32[1,256]{1,0:T(1,128)S(1)} %add.17), channel_id=1, source_target_pairs={{0,4},{1,5},{2,6},{3,7},{4,0},{5,1},{6,2},{7,3},{8,12},{9,13},{10,... | collective-permute-start | bytes 3080 | tf_op jit(solution)/shard_map/ppermute | solution.py:186
  46.0 4.5 %collective-permute-start.18 = (f32[1,256]{1,0:T(1,128)S(1)}, f32[1,256]{1,0:T(1,128)S(1)}, u32[]{:S(2)}, u32[]{:S(2)}) collective-permute-start(f32[1,256]{1,0:T(1,128)S(1)} %add.18), channel_id=1, source_target_pairs={{0,8},{1,9},{2,10},{3,11},{4,12},{5,13},{6,14},{7,15},{8,0},{9,1},... | collective-permute-start | bytes 3080 | tf_op jit(solution)/shard_map/ppermute | solution.py:186

commit v3 on v0

v3 whole, which is shorter than its diff:
```python
import functools

import jax
import jax.numpy as jnp
from jax import lax
from jax.experimental import pallas as pl
from jax.experimental.pallas import tpu as pltpu
from jax.sharding import PartitionSpec as P

SPLIT = (1024, 3072, 2048, 2048)
FETCH = 512
STEP = 1024
LANES = 128
GROUP = 16
TABLE_FLOPS = 2 * 10**10
GRANT = 8 << 20
VMEM = pl.BlockSpec(memory_space=pltpu.VMEM)
HBM = pl.BlockSpec(memory_space=pltpu.HBM)
ANY = pl.BlockSpec(memory_space=pl.ANY)


def place_of(units, unit):
    chips = units // 2
    chip = unit // 2
    if units != 16:
        return chip
    odd = chip % 2
    return (1 - odd) * (chip // 2) + odd * (chips - 1 - chip // 2)


def unit_at(units, place, core):
    chips = units // 2
    place = lax.rem(place + 2 * chips, chips)
    if units != 16:
        return 2 * place + core
    back = place // (chips // 2)
    return 2 * ((1 - back) * 2 * place + back * (2 * (chips - 1 - place) + 1)) + core


def block_of(units, hop, same, mine):
    unit = lax.axis_index("unit")
    core = lax.rem(unit, 2)
    holder = core if mine else 1 - core
    place = place_of(units, unit) - (1 - 2 * holder) * hop
    return unit_at(units, place, holder if same else 1 - holder)


def pairs_of(units):
    chips = units // 2
    walk = sorted(range(chips), key=lambda chip: place_of(units, 2 * chip))
    at = lambda place, core: 2 * walk[place % chips] + core
    ahead, across, twin = [], [], []
    for place in range(chips):
        for core, way in ((0, 1), (1, -1)):
            ahead.append((at(place, core), at(place + way, core)))
            across.append((at(place, 1 - core), at(place + way, core)))
            twin.append((at(place, core), at(place, 1 - core)))
    return ahead, across, twin


def product(rows, columns):
    return lax.dot_general(rows, columns, (((1,), (1,)), ((), ())), preferred_element_type=jnp.float32)


def fetches(q_ref, first, count, to, sems):
    return [
        pltpu.make_async_copy(
            q_ref.at[pl.ds(first + at, FETCH)], to.at[pl.ds(at, FETCH)], sems.at[at // FETCH]
        )
        for at in range(0, count, FETCH)
    ]


def first_kernel(width, following, x_ref, q_ref, x, weights, slab, own, placed, ready, coming):
    move = pltpu.make_async_copy(x_ref, x, placed)
    move.start()
    mine = fetches(q_ref, 0, width, own, ready)
    later = fetches(q_ref, width, following, slab, coming)
    for copy in mine + later:
        copy.start()
    move.wait()
    for index, copy in enumerate(mine):
        copy.wait()
        at = slice(index * FETCH, (index + 1) * FETCH)
        weights[:, at] = product(x[...], own[at, :])
    for copy in later:
        copy.wait()


def next_kernel(first, width, following, waits, x, q_ref, slab, *refs):
    weights = refs[waits]
    later = []
    if following:
        later = fetches(q_ref, first + width, following, refs[waits + 1], refs[-1])
    for copy in later:
        copy.start()

    @pl.loop(0, width // STEP)
    def _(i):
        at = pl.ds(pl.multiple_of(i * STEP, STEP), STEP)
        weights[:, at] = product(x[...], slab[at, :])

    for copy in later:
        copy.wait()


def weigh(piece, x, q, slab, after):
    tokens, depth = x.shape
    first, width = sum(SPLIT[:piece]), SPLIT[piece]
    following = SPLIT[piece + 1] if piece + 1 < len(SPLIT) else 0
    out_shape = [pltpu.VMEM((tokens, width), jnp.float32)]
    scratch = []
    if following:
        out_shape.append(pltpu.VMEM((following, depth), q.dtype))
        scratch = [pltpu.SemaphoreType.DMA((following // FETCH,))]
    if piece:
        kernel = functools.partial(next_kernel, first, width, following, len(after))
        operands = [x, q, slab, *after]
        in_specs = [VMEM, HBM, VMEM] + [ANY] * len(after)
    else:
        kernel = functools.partial(first_kernel, width, following)
        operands = [x, q]
        in_specs = [HBM, HBM]
        out_shape.insert(0, pltpu.VMEM(x.shape, x.dtype))
        scratch = [
            pltpu.VMEM((width, depth), q.dtype),
            pltpu.SemaphoreType.DMA,
            pltpu.SemaphoreType.DMA((width // FETCH,)),
        ] + scratch
    return pl.pallas_call(
        kernel,
        in_specs=in_specs,
        out_specs=[VMEM] * len(out_shape),
        out_shape=out_shape,
        scratch_shapes=scratch,
        compiler_params=pltpu.CompilerParams(vmem_limit_bytes=GRANT),
        cost_estimate=pl.CostEstimate(
            flops=2 * tokens * depth * width,
            bytes_accessed=2 * depth * width,
            transcendentals=0,
        ),
    )(*operands)


def dots(gradient, weights):
    total = jnp.zeros((gradient.shape[0], LANES), jnp.float32)
    at = 0
    for width, weight in zip(SPLIT, weights):
        for lane in range(0, width, LANES):
            total += gradient[:, at : at + LANES].astype(jnp.float32) * weight(lane)
            at += LANES
    return total


def rows_of(ref, start, block):
    return lambda lane: ref[pl.ds(start, block), lane : lane + LANES]


def stack_kernel(*refs):
    out, at = refs[-1], 0
    for ref in refs[:-1]:
        out[at : at + ref.shape[0], :] = ref[...]
        at += ref.shape[0]


def stack(arrays):
    rows = sum(array.shape[0] for array in arrays)
    return pl.pallas_call(
        stack_kernel,
        in_specs=[VMEM] * len(arrays),
        out_specs=VMEM,
        out_shape=jax.ShapeDtypeStruct((rows, arrays[0].shape[1]), arrays[0].dtype),
        compiler_params=pltpu.CompilerParams(vmem_limit_bytes=GRANT),
    )(*arrays)


def table_kernel(units, block, places, fresh, *refs):
    count = 1 + max(array for array, _, _ in places)
    gradients, weights, table = refs[:count], refs[count : count + len(SPLIT)], refs[-1]
    table[...] = jnp.zeros_like(table) if fresh else refs[-2][...]
    for array, row, place in places:
        start = pl.multiple_of(block_of(units, *place) * block, block)
        gradient = gradients[array][row : row + block, :]
        table[pl.ds(start, block), :] = dots(gradient, [rows_of(ref, start, block) for ref in weights])


def add_blocks(units, block, found, weights, table, flops):
    shape = (weights[0].shape[0], LANES)
    arrays, places = [], []
    for place, array, row in found:
        if not any(array is known for known in arrays):
            arrays.append(array)
        index = [array is known for known in arrays].index(True)
        places.append((index, row, place))
    extra = [] if table is None else [table]
    return pl.pallas_call(
        functools.partial(table_kernel, units, block, places, table is None),
        in_specs=[VMEM] * (len(arrays) + len(weights) + len(extra)),
        out_specs=VMEM,
        out_shape=jax.ShapeDtypeStruct(shape, jnp.float32),
        compiler_params=pltpu.CompilerParams(vmem_limit_bytes=GRANT),
        cost_estimate=pl.CostEstimate(flops=flops, bytes_accessed=0, transcendentals=0),
    )(*arrays, *weights, *extra)


def give_kernel(units, places, *refs):
    weights, out = refs[:-1], refs[-1]
    block = out.shape[0] // len(places)
    for index, place in enumerate(places):
        start = pl.multiple_of(block_of(units, *place, False) * block, block)
        at = 0
        for ref in weights:
            out[index * block : (index + 1) * block, at : at + ref.shape[1]] = ref[pl.ds(start, block), :]
            at += ref.shape[1]


def last_kernel(units, block, places, *refs):
    gradients, refs = refs[: len(places)], refs[len(places) :]
    theirs, table, *weights, out, full = refs
    full[...] = table[...]

    def rows(place):
        return pl.ds(pl.multiple_of(block_of(units, *place) * block, block), block)

    for index, (gradient, place) in enumerate(zip(gradients, places)):
        here = rows((*place, True))

        def weight(piece, index=index, here=here):
            at = sum(SPLIT[:piece])
            own = rows_of(weights[piece], here.start, block)
            other = lambda lane: theirs[index * block : (index + 1) * block, at + lane : at + lane + LANES]
            if index + 1 < len(places):
                return other
            return lambda lane: own(lane) + other(lane)

        full[here, :] += dots(gradient, [weight(piece) for piece in range(len(weights))])
    out[...] = jnp.sum(full[...].T, axis=0, keepdims=True)


def in_vmem(array):
    return pltpu.with_memory_space_constraint(array, pltpu.VMEM)


def body(units, query_grad, out_grads, inputs):
    ahead, across, twin = pairs_of(units)
    send = lambda value, pairs: lax.ppermute(value, "unit", pairs)
    block, outputs = out_grads.shape
    tokens = inputs.shape[0]

    weights = []
    q = pltpu.with_memory_space_constraint(query_grad, pltpu.HBM)
    state = [pltpu.with_memory_space_constraint(inputs, pltpu.HBM), None]

    def piece(*after):
        if len(weights) == len(SPLIT):
            return
        made = list(weigh(len(weights), state[0], q, state[1], after))
        if not weights:
            state[0] = in_vmem(made.pop(0))
        weights.append(in_vmem(made.pop(0)))
        state[1] = in_vmem(made[0]) if made else None

    def later(value):
        return lax.optimization_barrier((value, weights[-1]))[0]

    hops = units // 4
    held, places = [out_grads], [(0, True)]
    same, other = send(out_grads, ahead), send(out_grads, across)
    piece()
    for hop in range(1, hops):
        held += [same, other]
        places += [(hop, True), (hop, False)]
        if hop + 1 == hops:
            last = send(later(same), ahead)
            break
        next_same = send(later(same), ahead)
        if hop > 1:
            piece(same)
        next_other = send(later(other) if hop > 1 else other, ahead)
        if hop == 1:
            piece(same, other)
        else:
            piece(other)
        same, other = next_same, next_other

    ends = places[-1:] + [(hops, True)]
    theirs = pl.pallas_call(
        functools.partial(give_kernel, units, ends),
        in_specs=[VMEM] * len(weights),
        out_specs=VMEM,
        out_shape=jax.ShapeDtypeStruct((len(ends) * block, outputs), jnp.float32),
        compiler_params=pltpu.CompilerParams(vmem_limit_bytes=GRANT),
    )(*weights)
    theirs = send(theirs, twin)
    given = send(stack([lax.optimization_barrier((out_grads, weights[2]))[0]] + held[1:-2]), twin)
    more = send(held[-2], twin)

    mine = [((*place, True), array, 0) for place, array in zip(places, held)]
    others = [((*place, False), given, index * block) for index, place in enumerate(places[:-2])]
    others.append(((*places[-2], False), more, 0))
    table = None
    for found, flops in ((mine, TABLE_FLOPS), (others, 0)):
        for group in range(0, len(found), GROUP):
            table = add_blocks(units, block, found[group : group + GROUP], weights, table, flops)
    partial_value = pl.pallas_call(
        functools.partial(last_kernel, units, block, ends),
        in_specs=[VMEM] * (4 + len(weights)),
        out_specs=VMEM,
        out_shape=jax.ShapeDtypeStruct((1, tokens), jnp.float32),
        scratch_shapes=[pltpu.VMEM((tokens, LANES), jnp.float32)],
        compiler_params=pltpu.CompilerParams(vmem_limit_bytes=GRANT),
    )(held[-1], last, theirs, table, *weights)

    bit = 1
    while bit < units:
        pairs = [(unit, unit ^ bit) for unit in range(units)]
        partial_value += send(partial_value, pairs)
        bit *= 2
    return partial_value.reshape(tokens)


def solution(mesh):
    return jax.shard_map(
        functools.partial(body, mesh.shape["unit"]),
        mesh=mesh,
        in_specs=(P("job", "unit"), P(("job", "unit"), None), P("job", "unit")),
        out_specs=P("job"),
        check_vma=False,
    )
```

time: 117 us -> 47.1 us (0.40)
  waiting for transfers between devices: 56.3 us -> 15.3 us
  blocking collectives: 31.7 us -> 0 us
  Pallas kernels: 0 us -> 16 us
  matrix products: 15 us -> 0 us
  starting transfers between devices: 0.01 us -> 15 us
  between operations: 13.4 us -> 0.1 us
    all_gather x1 -> x0, waiting for transfers between devices: 55.6 us -> none  [body(): lax.all_gather(out_grads, 'unit', axis=0, tiled=True)]
    psum x1 -> x0, blocking collectives: 31.7 us -> none  [body(): return lax.psum(partial_value, 'unit')]
    pallas_call x0 -> x9, Pallas kernels: none -> 16 us  [the longest x4 14.8 us: weigh(): pl.pallas_call(kernel, in_specs=in_specs, out_specs=[VMEM] * len(out_shap...]
    ppermute x0 -> x14, waiting for transfers between devices: none -> 15.3 us  [body(): send = lambda value, pairs: lax.ppermute(value, 'unit', pairs)]
    dot_general x1 -> x0, matrix products: 15 us -> none  [body(): jnp.dot(lax.all_gather(out_grads, 'unit', axis=0, tiled=True), query_grad...]
    ppermute x0 -> x14, starting transfers between devices: none -> 15 us  [body(): send = lambda value, pairs: lax.ppermute(value, 'unit', pairs)]
  transfers between devices with their start and end apart: 1 -> 14, of which waited for: 1 -> 8; matrix products, arithmetic and copies ran while one was open for 0% -> 0% of each run, Pallas kernels for 0% -> 34%
where the time goes in v3:
time: 47.1 us; the launch traced here: 47 us
  Pallas kernels  16 us (34%)
  waiting for transfers between devices  15.3 us (32%)
  starting transfers between devices  15 us (32%)
  other arithmetic  0.57 us (1%)
    ppermute x14, waiting for transfers between devices, body(): send = lambda value, pairs: lax.ppermute(value, 'unit', pairs)  15.3 us
    ppermute x14, starting transfers between devices, body(): send = lambda value, pairs: lax.ppermute(value, 'unit', pairs)  15 us
    pallas_call x4, Pallas kernels, weigh(): pl.pallas_call(kernel, in_specs=in_specs, out_specs=[VMEM] * len(out_shap...  14.8 us
  transfers between devices with their start and end apart: 14, of which 8 were waited for; matrix products, arithmetic and copies ran while one was open for 0% of the time, Pallas kernels for 34%

profile of v3, /device:TPU:0, one launch (start us, length us, event | category | flops | bytes accessed | tf_op | source)
XLA Modules:
  0.0 47.0 jit_solution(2908871846032992397)
XLA Ops:
  0.0 3.0 %collective-permute-start.2 = (bf16[16,8192]{1,0:T(8,128)(2,1)}, bf16[16,8192]{1,0:T(8,128)(2,1)S(1)}, u32[]{:S(2)}, u32[]{:S(2)}) collective-permute-start(bf16[16,8192]{1,0:T(8,128)(2,1)} %refs_0_.2), channel_id=1, source_target_pairs={{0,4},{1,3},{4,8},{5,1},{8,12},{9,5},{12,14},{13,9},{14,10},{15,13... | collective-permute-start | bytes 786440 | tf_op jit(solution)/shard_map/ppermute | solution.py:246
  3.0 0.7 %collective-permute-start = (bf16[16,8192]{1,0:T(8,128)(2,1)}, bf16[16,8192]{1,0:T(8,128)(2,1)S(1)}, u32[]{:S(2)}, u32[]{:S(2)}) collective-permute-start(bf16[16,8192]{1,0:T(8,128)(2,1)} %refs_0_.2), channel_id=1, source_target_pairs={{1,4},{0,3},{5,8},{4,1},{9,12},{8,5},{13,14},{12,9},{15,10},{14,13... | collective-permute-start | bytes 786440 | tf_op jit(solution)/shard_map/ppermute | solution.py:246
  3.7 5.8 %shard_map.37 = (bf16[256,1792]{1,0:T(8,128)(2,1)S(1)}, f32[256,1024]{1,0:T(8,128)S(1)}, bf16[3072,1792]{1,0:T(8,128)(2,1)S(1)}) custom-call(bf16[256,1792]{1,0:T(8,128)(2,1)} %x_ref.1, bf16[8192,1792]{1,0:T(8,128)(2,1)} %q_ref.7), custom_call_target="tpu_custom_call" | custom-call | flops 939524096 | bytes 3670016 | tf_op jit(solution)/shard_map/pallas_call | solution.py:130
  9.5 0.0 collective-permute-done.2.refs_0_.refs_1_
  9.5 1.9 %collective-permute-start.3 = (bf16[16,8192]{1,0:T(8,128)(2,1)S(1)}, bf16[16,8192]{1,0:T(8,128)(2,1)S(1)}, u32[]{:S(2)}, u32[]{:S(2)}) collective-permute-start(bf16[16,8192]{1,0:T(8,128)(2,1)S(1)} %collective-permute-done.2.refs_0_.refs_1_), channel_id=1, source_target_pairs={{0,4},{1,3},{4,8},{5,1},{8,12},{9,5},{12,14},{13,9},{14,10},{15,13... | collective-permute-start | bytes 786440 | tf_op jit(solution)/shard_map/ppermute | solution.py:246
  11.4 0.0 collective-permute-done.refs_1_.refs_2_
  11.4 1.6 %collective-permute-start.1 = (bf16[16,8192]{1,0:T(8,128)(2,1)S(1)}, bf16[16,8192]{1,0:T(8,128)(2,1)S(1)}, u32[]{:S(2)}, u32[]{:S(2)}) collective-permute-start(bf16[16,8192]{1,0:T(8,128)(2,1)S(1)} %collective-permute-done.refs_1_.refs_2_), channel_id=1, source_target_pairs={{0,4},{1,3},{4,8},{5,1},{8,12},{9,5},{12,14},{13,9},{14,10},{15,13... | collective-permute-start | bytes 786440 | tf_op jit(solution)/shard_map/ppermute | solution.py:246
  13.0 3.5 %shard_map.38 = (f32[256,3072]{1,0:T(8,128)S(1)}, bf16[2048,1792]{1,0:T(8,128)(2,1)S(1)}) custom-call(bf16[256,1792]{1,0:T(8,128)(2,1)S(1)} %get-tuple-element.17.x, bf16[8192,1792]{1,0:T(8,128)(2,1)} %q_ref.7, bf16[3072,1792]{1,0:T(8,128)(2,1)S(1)} %get-tuple-element.18.slab, bf16[16,8192]{1,0:T(8,128)(2,1)S(1)} %collective-permute-done.2.refs_0_.refs_1_, ...), custom_call_target="tpu_custom_call" | custom-call | flops 2818572288 | bytes 11010048 | tf_op jit(solution)/shard_map/pallas_call | solution.py:130
  16.5 0.2 collective-permute-done.3.refs_0_.refs_3_
  16.7 1.5 %collective-permute-start.5 = (bf16[16,8192]{1,0:T(8,128)(2,1)S(1)}, bf16[16,8192]{1,0:T(8,128)(2,1)S(1)}, u32[]{:S(2)}, u32[]{:S(2)}) collective-permute-start(bf16[16,8192]{1,0:T(8,128)(2,1)S(1)} %collective-permute-done.3.refs_0_.refs_3_), channel_id=1, source_target_pairs={{0,4},{1,3},{4,8},{5,1},{8,12},{9,5},{12,14},{13,9},{14,10},{15,13... | collective-permute-start | bytes 786440 | tf_op jit(solution)/shard_map/ppermute | solution.py:246
  18.2 0.0 copy-start
  18.2 3.2 %shard_map.39 = (f32[256,2048]{1,0:T(8,128)S(1)}, bf16[2048,1792]{1,0:T(8,128)(2,1)S(1)}) custom-call(bf16[256,1792]{1,0:T(8,128)(2,1)S(1)} %get-tuple-element.17.x, bf16[8192,1792]{1,0:T(8,128)(2,1)} %q_ref.7, bf16[2048,1792]{1,0:T(8,128)(2,1)S(1)} %get-tuple-element.19.slab, bf16[16,8192]{1,0:T(8,128)(2,1)S(1)} %collective-permute-done.3.refs_0_.refs_3_), custom_call_target="tpu_custom_call" | custom-call | flops 1879048192 | bytes 7340032 | tf_op jit(solution)/shard_map/pallas_call | solution.py:130
  21.4 0.0 collective-permute-done.1.refs_0_.refs_4_
  21.4 2.4 %collective-permute-start.4 = (bf16[16,8192]{1,0:T(8,128)(2,1)S(1)}, bf16[16,8192]{1,0:T(8,128)(2,1)S(1)}, u32[]{:S(2)}, u32[]{:S(2)}) collective-permute-start(bf16[16,8192]{1,0:T(8,128)(2,1)S(1)} %collective-permute-done.1.refs_0_.refs_4_), channel_id=1, source_target_pairs={{0,4},{1,3},{4,8},{5,1},{8,12},{9,5},{12,14},{13,9},{14,10},{15,13... | collective-permute-start | bytes 786440 | tf_op jit(solution)/shard_map/ppermute | solution.py:246
  23.8 0.0 copy-done
  23.8 0.1 shard_map.42
  23.9 0.1 collective-permute-start.8
  24.0 2.3 %shard_map.40.refs_3_.refs_10_.refs_5_.refs_7_ = f32[256,2048]{1,0:T(8,128)S(1)} custom-call(bf16[256,1792]{1,0:T(8,128)(2,1)S(1)} %get-tuple-element.17.x, bf16[8192,1792]{1,0:T(8,128)(2,1)} %q_ref.7, bf16[2048,1792]{1,0:T(8,128)(2,1)S(1)} %get-tuple-element.26.slab, bf16[16,8192]{1,0:T(8,128)(2,1)S(1)} %collective-permute-done.1.refs_0_.refs_4_), custom_call_target="tpu_custom_call" | custom-call | flops 1879048192 | bytes 7340032 | tf_op jit(solution)/shard_map/pallas_call | solution.py:130
  26.3 0.1 shard_map.41
  26.4 0.6 %collective-permute-start.7 = (f32[32,8192]{1,0:T(8,128)S(1)}, f32[32,8192]{1,0:T(8,128)S(1)}, u32[]{:S(2)}, u32[]{:S(2)}) collective-permute-start(f32[32,8192]{1,0:T(8,128)S(1)} %shard_map.41), channel_id=1, source_target_pairs={{0,1},{1,0},{4,5},{5,4},{8,9},{9,8},{12,13},{13,12},{14,15},{15,14... | collective-permute-start | bytes 3145736 | tf_op jit(solution)/shard_map/ppermute | solution.py:246
  27.0 0.0 collective-permute-done.5.refs_5_
  27.0 0.5 %collective-permute-start.6 = (bf16[16,8192]{1,0:T(8,128)(2,1)S(1)}, bf16[16,8192]{1,0:T(8,128)(2,1)S(1)}, u32[]{:S(2)}, u32[]{:S(2)}) collective-permute-start(bf16[16,8192]{1,0:T(8,128)(2,1)S(1)} %collective-permute-done.5.refs_5_), channel_id=1, source_target_pairs={{0,4},{1,3},{4,8},{5,1},{8,12},{9,5},{12,14},{13,9},{14,10},{15,13... | collective-permute-start | bytes 786440 | tf_op jit(solution)/shard_map/ppermute | solution.py:246
  27.4 0.0 collective-permute-start.9
  27.4 0.4 collective-permute-done.4.refs_6_.refs_0_
  27.8 0.4 shard_map.43.refs_6_
  28.3 1.4 %collective-permute-done.9.refs_1_ = bf16[16,8192]{1,0:T(8,128)(2,1)S(1)} collective-permute-done((bf16[16,8192]{1,0:T(8,128)(2,1)S(1)}, bf16[16,8192]{1,0:T(8,128)(2,1)S(1)}, u32[]{:S(2)}, u32[]{:S(2)}) %collective-permute-start.9) | collective-permute-done | bytes 262176 | tf_op jit(solution)/shard_map/ppermute | solution.py:246
  29.6 0.0 collective-permute-done.8.refs_0_
  29.6 0.4 shard_map.44.refs_3_
  30.0 3.4 %collective-permute-done.6.refs_1_ = bf16[16,8192]{1,0:T(8,128)(2,1)S(1)} collective-permute-done((bf16[16,8192]{1,0:T(8,128)(2,1)S(1)}, bf16[16,8192]{1,0:T(8,128)(2,1)S(1)}, u32[]{:S(2)}, u32[]{:S(2)}) %collective-permute-start.6) | collective-permute-done | bytes 262176 | tf_op jit(solution)/shard_map/ppermute | solution.py:246
  33.3 0.0 collective-permute-done.7.refs_2_
  33.3 0.2 shard_map.45
  33.6 0.1 collective-permute-start.10
  33.7 1.1 %collective-permute-done.10 = f32[1,256]{1,0:T(1,128)S(1)} collective-permute-done((f32[1,256]{1,0:T(1,128)S(1)}, f32[1,256]{1,0:T(1,128)S(1)}, u32[]{:S(2)}, u32[]{:S(2)}) %collective-permute-start.10) | collective-permute-done | bytes 1056 | tf_op jit(solution)/shard_map/ppermute | solution.py:246
  34.8 0.0 collective-permute-start.11
  34.8 3.6 %collective-permute-done.11 = f32[1,256]{1,0:T(1,128)S(1)} collective-permute-done((f32[1,256]{1,0:T(1,128)S(1)}, f32[1,256]{1,0:T(1,128)S(1)}, u32[]{:S(2)}, u32[]{:S(2)}) %collective-permute-start.11) | collective-permute-done | bytes 1056 | tf_op jit(solution)/shard_map/ppermute | solution.py:246
  38.4 0.5 %collective-permute-start.12 = (f32[1,256]{1,0:T(1,128)S(1)}, f32[1,256]{1,0:T(1,128)S(1)}, u32[]{:S(2)}, u32[]{:S(2)}) collective-permute-start(f32[1,256]{1,0:T(1,128)S(1)} %add.13), channel_id=1, source_target_pairs={{0,4},{1,5},{2,6},{3,7},{4,0},{5,1},{6,2},{7,3},{8,12},{9,13},{10,... | collective-permute-start | bytes 3080 | tf_op jit(solution)/shard_map/ppermute | solution.py:246
  38.8 3.1 %collective-permute-done.12 = f32[1,256]{1,0:T(1,128)S(1)} collective-permute-done((f32[1,256]{1,0:T(1,128)S(1)}, f32[1,256]{1,0:T(1,128)S(1)}, u32[]{:S(2)}, u32[]{:S(2)}) %collective-permute-start.12) | collective-permute-done | bytes 1056 | tf_op jit(solution)/shard_map/ppermute | solution.py:246
  41.9 2.3 %collective-permute-start.13 = (f32[1,256]{1,0:T(1,128)S(1)}, f32[1,256]{1,0:T(1,128)S(1)}, u32[]{:S(2)}, u32[]{:S(2)}) collective-permute-start(f32[1,256]{1,0:T(1,128)S(1)} %add.14), channel_id=1, source_target_pairs={{0,8},{1,9},{2,10},{3,11},{4,12},{5,13},{6,14},{7,15},{8,0},{9,1},... | collective-permute-start | bytes 3080 | tf_op jit(solution)/shard_map/ppermute | solution.py:246
  44.2 2.2 %collective-permute-done.13 = f32[1,256]{1,0:T(1,128)S(1)} collective-permute-done((f32[1,256]{1,0:T(1,128)S(1)}, f32[1,256]{1,0:T(1,128)S(1)}, u32[]{:S(2)}, u32[]{:S(2)}) %collective-permute-start.13) | collective-permute-done | bytes 1056 | tf_op jit(solution)/shard_map/ppermute | solution.py:246
  46.4 0.6 %add.15 = f32[1,256]{1,0:T(1,128)} add(f32[1,256]{1,0:T(1,128)S(1)} %add.14, f32[1,256]{1,0:T(1,128)S(1)} %collective-permute-done.13) | non-fusion elementwise | flops 256 | bytes 3072 | tf_op jit(solution)/shard_map/add | solution.py:317
  (3 shorter events, 0.0 us)
Async XLA Ops:
  0.0 9.5 %collective-permute-start.2 = (bf16[16,8192]{1,0:T(8,128)(2,1)}, bf16[16,8192]{1,0:T(8,128)(2,1)S(1)}, u32[]{:S(2)}, u32[]{:S(2)}) collective-permute-start(bf16[16,8192]{1,0:T(8,128)(2,1)} %refs_0_.2), channel_id=1, source_target_pairs={{0,4},{1,3},{4,8},{5,1},{8,12},{9,5},{12,14},{13,9},{14,10},{15,13... | collective-permute-start | bytes 786440 | tf_op jit(solution)/shard_map/ppermute | solution.py:246
  3.0 8.4 %collective-permute-start = (bf16[16,8192]{1,0:T(8,128)(2,1)}, bf16[16,8192]{1,0:T(8,128)(2,1)S(1)}, u32[]{:S(2)}, u32[]{:S(2)}) collective-permute-start(bf16[16,8192]{1,0:T(8,128)(2,1)} %refs_0_.2), channel_id=1, source_target_pairs={{1,4},{0,3},{5,8},{4,1},{9,12},{8,5},{13,14},{12,9},{15,10},{14,13... | collective-permute-start | bytes 786440 | tf_op jit(solution)/shard_map/ppermute | solution.py:246
  9.5 7.1 %collective-permute-start.3 = (bf16[16,8192]{1,0:T(8,128)(2,1)S(1)}, bf16[16,8192]{1,0:T(8,128)(2,1)S(1)}, u32[]{:S(2)}, u32[]{:S(2)}) collective-permute-start(bf16[16,8192]{1,0:T(8,128)(2,1)S(1)} %collective-permute-done.2.refs_0_.refs_1_), channel_id=1, source_target_pairs={{0,4},{1,3},{4,8},{5,1},{8,12},{9,5},{12,14},{13,9},{14,10},{15,13... | collective-permute-start | bytes 786440 | tf_op jit(solution)/shard_map/ppermute | solution.py:246
  11.4 10.0 %collective-permute-start.1 = (bf16[16,8192]{1,0:T(8,128)(2,1)S(1)}, bf16[16,8192]{1,0:T(8,128)(2,1)S(1)}, u32[]{:S(2)}, u32[]{:S(2)}) collective-permute-start(bf16[16,8192]{1,0:T(8,128)(2,1)S(1)} %collective-permute-done.refs_1_.refs_2_), channel_id=1, source_target_pairs={{0,4},{1,3},{4,8},{5,1},{8,12},{9,5},{12,14},{13,9},{14,10},{15,13... | collective-permute-start | bytes 786440 | tf_op jit(solution)/shard_map/ppermute | solution.py:246
  16.7 10.3 %collective-permute-start.5 = (bf16[16,8192]{1,0:T(8,128)(2,1)S(1)}, bf16[16,8192]{1,0:T(8,128)(2,1)S(1)}, u32[]{:S(2)}, u32[]{:S(2)}) collective-permute-start(bf16[16,8192]{1,0:T(8,128)(2,1)S(1)} %collective-permute-done.3.refs_0_.refs_3_), channel_id=1, source_target_pairs={{0,4},{1,3},{4,8},{5,1},{8,12},{9,5},{12,14},{13,9},{14,10},{15,13... | collective-permute-start | bytes 786440 | tf_op jit(solution)/shard_map/ppermute | solution.py:246
  18.2 5.6 %copy-start = (bf16[16,8192]{1,0:T(8,128)(2,1)S(1)}, bf16[16,8192]{1,0:T(8,128)(2,1)}, u32[]{:S(2)}) copy-start(bf16[16,8192]{1,0:T(8,128)(2,1)} %refs_0_.2) | copy-start | bytes 786436
  21.4 6.4 %collective-permute-start.4 = (bf16[16,8192]{1,0:T(8,128)(2,1)S(1)}, bf16[16,8192]{1,0:T(8,128)(2,1)S(1)}, u32[]{:S(2)}, u32[]{:S(2)}) collective-permute-start(bf16[16,8192]{1,0:T(8,128)(2,1)S(1)} %collective-permute-done.1.refs_0_.refs_4_), channel_id=1, source_target_pairs={{0,4},{1,3},{4,8},{5,1},{8,12},{9,5},{12,14},{13,9},{14,10},{15,13... | collective-permute-start | bytes 786440 | tf_op jit(solution)/shard_map/ppermute | solution.py:246
  23.9 5.7 %collective-permute-start.8 = (bf16[80,8192]{1,0:T(8,128)(2,1)S(1)}, bf16[80,8192]{1,0:T(8,128)(2,1)S(1)}, u32[]{:S(2)}, u32[]{:S(2)}) collective-permute-start(bf16[80,8192]{1,0:T(8,128)(2,1)S(1)} %shard_map.42), channel_id=1, source_target_pairs={{0,1},{1,0},{4,5},{5,4},{8,9},{9,8},{12,13},{13,12},{14,15},{15,14... | collective-permute-start | bytes 3932168 | tf_op jit(solution)/shard_map/ppermute | solution.py:246
  26.4 6.9 %collective-permute-start.7 = (f32[32,8192]{1,0:T(8,128)S(1)}, f32[32,8192]{1,0:T(8,128)S(1)}, u32[]{:S(2)}, u32[]{:S(2)}) collective-permute-start(f32[32,8192]{1,0:T(8,128)S(1)} %shard_map.41), channel_id=1, source_target_pairs={{0,1},{1,0},{4,5},{5,4},{8,9},{9,8},{12,13},{13,12},{14,15},{15,14... | collective-permute-start | bytes 3145736 | tf_op jit(solution)/shard_map/ppermute | solution.py:246
  27.0 6.4 %collective-permute-start.6 = (bf16[16,8192]{1,0:T(8,128)(2,1)S(1)}, bf16[16,8192]{1,0:T(8,128)(2,1)S(1)}, u32[]{:S(2)}, u32[]{:S(2)}) collective-permute-start(bf16[16,8192]{1,0:T(8,128)(2,1)S(1)} %collective-permute-done.5.refs_5_), channel_id=1, source_target_pairs={{0,4},{1,3},{4,8},{5,1},{8,12},{9,5},{12,14},{13,9},{14,10},{15,13... | collective-permute-start | bytes 786440 | tf_op jit(solution)/shard_map/ppermute | solution.py:246
  27.4 2.2 %collective-permute-start.9 = (bf16[16,8192]{1,0:T(8,128)(2,1)S(1)}, bf16[16,8192]{1,0:T(8,128)(2,1)S(1)}, u32[]{:S(2)}, u32[]{:S(2)}) collective-permute-start(bf16[16,8192]{1,0:T(8,128)(2,1)S(1)} %collective-permute-done.5.refs_5_), channel_id=1, source_target_pairs={{0,1},{1,0},{4,5},{5,4},{8,9},{9,8},{12,13},{13,12},{14,15},{15,14... | collective-permute-start | bytes 786440 | tf_op jit(solution)/shard_map/ppermute | solution.py:246
  33.6 1.2 %collective-permute-start.10 = (f32[1,256]{1,0:T(1,128)S(1)}, f32[1,256]{1,0:T(1,128)S(1)}, u32[]{:S(2)}, u32[]{:S(2)}) collective-permute-start(f32[1,256]{1,0:T(1,128)S(1)} %shard_map.45), channel_id=1, source_target_pairs={{0,1},{1,0},{2,3},{3,2},{4,5},{5,4},{6,7},{7,6},{8,9},{9,8},{10,11... | collective-permute-start | bytes 3080 | tf_op jit(solution)/shard_map/ppermute | solution.py:246
  34.8 3.6 %collective-permute-start.11 = (f32[1,256]{1,0:T(1,128)S(1)}, f32[1,256]{1,0:T(1,128)S(1)}, u32[]{:S(2)}, u32[]{:S(2)}) collective-permute-start(f32[1,256]{1,0:T(1,128)S(1)} %add.12), channel_id=1, source_target_pairs={{0,2},{1,3},{2,0},{3,1},{4,6},{5,7},{6,4},{7,5},{8,10},{9,11},{10,... | collective-permute-start | bytes 3080 | tf_op jit(solution)/shard_map/ppermute | solution.py:246
  38.4 3.6 %collective-permute-start.12 = (f32[1,256]{1,0:T(1,128)S(1)}, f32[1,256]{1,0:T(1,128)S(1)}, u32[]{:S(2)}, u32[]{:S(2)}) collective-permute-start(f32[1,256]{1,0:T(1,128)S(1)} %add.13), channel_id=1, source_target_pairs={{0,4},{1,5},{2,6},{3,7},{4,0},{5,1},{6,2},{7,3},{8,12},{9,13},{10,... | collective-permute-start | bytes 3080 | tf_op jit(solution)/shard_map/ppermute | solution.py:246
  41.9 4.5 %collective-permute-start.13 = (f32[1,256]{1,0:T(1,128)S(1)}, f32[1,256]{1,0:T(1,128)S(1)}, u32[]{:S(2)}, u32[]{:S(2)}) collective-permute-start(f32[1,256]{1,0:T(1,128)S(1)} %add.14), channel_id=1, source_target_pairs={{0,8},{1,9},{2,10},{3,11},{4,12},{5,13},{6,14},{7,15},{8,0},{9,1},... | collective-permute-start | bytes 3080 | tf_op jit(solution)/shard_map/ppermute | solution.py:246

commit v4 on v3

--- a/solution.py
+++ b/solution.py
@@ -7,12 +7,12 @@
 from jax.experimental.pallas import tpu as pltpu
 from jax.sharding import PartitionSpec as P
 
-SPLIT = (1024, 3072, 2048, 2048)
+SPLIT = (1024, 3072, 2560, 1536)
 FETCH = 512
-STEP = 1024
+STEP = 1280
 LANES = 128
 GROUP = 16
-TABLE_FLOPS = 2 * 10**10
+HIDDEN_FLOPS = 2 * 10**10
 GRANT = 8 << 20
 VMEM = pl.BlockSpec(memory_space=pltpu.VMEM)
 HBM = pl.BlockSpec(memory_space=pltpu.HBM)
@@ -41,21 +41,25 @@
     unit = lax.axis_index("unit")
     core = lax.rem(unit, 2)
     holder = core if mine else 1 - core
-    place = place_of(units, unit) - (1 - 2 * holder) * hop
-    return unit_at(units, place, holder if same else 1 - holder)
+    place = place_of(units, unit)
+    if hop == 0:
+        return unit_at(units, place, holder)
+    behind = 1 - lax.rem(holder + hop, 2)
+    return unit_at(units, place + (1 - 2 * behind) * hop, 1 - behind if same else behind)
 
 
 def pairs_of(units):
     chips = units // 2
     walk = sorted(range(chips), key=lambda chip: place_of(units, 2 * chip))
     at = lambda place, core: 2 * walk[place % chips] + core
-    ahead, across, twin = [], [], []
+    ahead, beside, twin = ([], []), [], []
     for place in range(chips):
         for core, way in ((0, 1), (1, -1)):
-            ahead.append((at(place, core), at(place + way, core)))
-            across.append((at(place, 1 - core), at(place + way, core)))
+            ahead[1].append((at(place, core), at(place + way, 1 - core)))
+            ahead[0].append((at(place, core), at(place - way, 1 - core)))
+            beside.append((at(place, 1 - core), at(place + way, 1 - core)))
             twin.append((at(place, core), at(place, 1 - core)))
-    return ahead, across, twin
+    return ahead, beside, twin
 
 
 def product(rows, columns):
@@ -95,9 +99,11 @@
     for copy in later:
         copy.start()
 
-    @pl.loop(0, width // STEP)
+    step = max(step for step in range(LANES, STEP + 1, LANES) if width % step == 0)
+
+    @pl.loop(0, width // step)
     def _(i):
-        at = pl.ds(pl.multiple_of(i * STEP, STEP), STEP)
+        at = pl.ds(pl.multiple_of(i * step, step), step)
         weights[:, at] = product(x[...], slab[at, :])
 
     for copy in later:
@@ -184,7 +190,7 @@
         table[pl.ds(start, block), :] = dots(gradient, [rows_of(ref, start, block) for ref in weights])
 
 
-def add_blocks(units, block, found, weights, table, flops):
+def add_blocks(units, block, found, weights, table):
     shape = (weights[0].shape[0], LANES)
     arrays, places = [], []
     for place, array, row in found:
@@ -199,7 +205,7 @@
         out_specs=VMEM,
         out_shape=jax.ShapeDtypeStruct(shape, jnp.float32),
         compiler_params=pltpu.CompilerParams(vmem_limit_bytes=GRANT),
-        cost_estimate=pl.CostEstimate(flops=flops, bytes_accessed=0, transcendentals=0),
+        cost_estimate=pl.CostEstimate(flops=0, bytes_accessed=0, transcendentals=0),
     )(*arrays, *weights, *extra)
 
 
@@ -214,14 +220,23 @@
             at += ref.shape[1]
 
 
-def last_kernel(units, block, places, *refs):
+def arrival_kernel(last, table, out):
+    out[...] = jnp.zeros_like(out)
+
+
+def last_kernel(units, block, places, mores, arrived, *refs):
     gradients, refs = refs[: len(places)], refs[len(places) :]
-    theirs, table, *weights, out, full = refs
+    given, more, theirs, table, *weights, out, full = refs
     full[...] = table[...]
 
     def rows(place):
         return pl.ds(pl.multiple_of(block_of(units, *place) * block, block), block)
 
+    for index, place in enumerate(mores):
+        here = rows((*place, False))
+        late = index + 1 == len(mores)
+        gradient = more[...] if late else given[index * block : (index + 1) * block, :]
+        full[here, :] = dots(gradient, [rows_of(ref, here.start, block) for ref in weights])
     for index, (gradient, place) in enumerate(zip(gradients, places)):
         here = rows((*place, True))
 
@@ -242,7 +257,7 @@
 
 
 def body(units, query_grad, out_grads, inputs):
-    ahead, across, twin = pairs_of(units)
+    ahead, beside, twin = pairs_of(units)
     send = lambda value, pairs: lax.ppermute(value, "unit", pairs)
     block, outputs = out_grads.shape
     tokens = inputs.shape[0]
@@ -265,22 +280,21 @@
 
     hops = units // 4
     held, places = [out_grads], [(0, True)]
-    same, other = send(out_grads, ahead), send(out_grads, across)
+    same, other = send(out_grads, ahead[1]), send(out_grads, beside)
     piece()
     for hop in range(1, hops):
         held += [same, other]
         places += [(hop, True), (hop, False)]
         if hop + 1 == hops:
-            last = send(later(same), ahead)
+            last = send(same, ahead[hops % 2])
+            piece(same)
             break
-        next_same = send(later(same), ahead)
+        next_same = send(later(same), ahead[(hop + 1) % 2])
         if hop > 1:
             piece(same)
-        next_other = send(later(other) if hop > 1 else other, ahead)
+        next_other = send(later(other) if hop > 1 else other, ahead[(hop + 1) % 2])
         if hop == 1:
             piece(same, other)
-        else:
-            piece(other)
         same, other = next_same, next_other
 
     ends = places[-1:] + [(hops, True)]
@@ -295,25 +309,30 @@
     given = send(stack([lax.optimization_barrier((out_grads, weights[2]))[0]] + held[1:-2]), twin)
     more = send(held[-2], twin)
 
-    mine = [((*place, True), array, 0) for place, array in zip(places, held)]
-    others = [((*place, False), given, index * block) for index, place in enumerate(places[:-2])]
-    others.append(((*places[-2], False), more, 0))
+    found = [((*place, True), array, 0) for place, array in zip(places, held)]
     table = None
-    for found, flops in ((mine, TABLE_FLOPS), (others, 0)):
-        for group in range(0, len(found), GROUP):
-            table = add_blocks(units, block, found[group : group + GROUP], weights, table, flops)
+    for group in range(0, len(found), GROUP):
+        table = add_blocks(units, block, found[group : group + GROUP], weights, table)
+    arrived = pl.pallas_call(
+        arrival_kernel,
+        in_specs=[ANY, ANY],
+        out_specs=VMEM,
+        out_shape=jax.ShapeDtypeStruct((8, LANES), jnp.float32),
+        compiler_params=pltpu.CompilerParams(vmem_limit_bytes=GRANT),
+        cost_estimate=pl.CostEstimate(flops=HIDDEN_FLOPS, bytes_accessed=0, transcendentals=0),
+    )(last, table)
     partial_value = pl.pallas_call(
-        functools.partial(last_kernel, units, block, ends),
-        in_specs=[VMEM] * (4 + len(weights)),
+        functools.partial(last_kernel, units, block, ends, places[:-1]),
+        in_specs=[ANY] + [VMEM] * (6 + len(weights)),
         out_specs=VMEM,
         out_shape=jax.ShapeDtypeStruct((1, tokens), jnp.float32),
         scratch_shapes=[pltpu.VMEM((tokens, LANES), jnp.float32)],
         compiler_params=pltpu.CompilerParams(vmem_limit_bytes=GRANT),
-    )(held[-1], last, theirs, table, *weights)
+    )(arrived, held[-1], last, given, more, theirs, table, *weights)
 
     bit = 1
     while bit < units:
-        pairs = [(unit, unit ^ bit) for unit in range(units)]
+        pairs = [(unit, unit ^ bit ^ (bit > 1)) for unit in range(units)]
         partial_value += send(partial_value, pairs)
         bit *= 2
     return partial_value.reshape(tokens)

time: 47.1 us -> 41.3 us (0.88)
  waiting for transfers between devices: 15.3 us -> 9.64 us
  Pallas kernels: 16 us -> 15.4 us
    ppermute x14, waiting for transfers between devices: 15.3 us -> 9.64 us  [body(): send = lambda value, pairs: lax.ppermute(value, 'unit', pairs)]
    pallas_call x4, Pallas kernels: 14.8 us -> 14.1 us  [weigh(): pl.pallas_call(kernel, in_specs=in_specs, out_specs=[VMEM] * len(out_shap...]
  transfers between devices with their start and end apart: 14 -> 14, of which waited for: 8 -> 8; matrix products, arithmetic and copies ran while one was open for 0% -> 0% of each run, Pallas kernels for 34% -> 36%
where the time goes in v4:
time: 41.3 us; the launch traced here: 41.2 us
  starting transfers between devices  15.4 us (37%)
  Pallas kernels  15.4 us (37%)
  waiting for transfers between devices  9.64 us (23%)
  other arithmetic  0.57 us (1%)
    ppermute x14, starting transfers between devices, body(): send = lambda value, pairs: lax.ppermute(value, 'unit', pairs)  15.4 us
    pallas_call x4, Pallas kernels, weigh(): pl.pallas_call(kernel, in_specs=in_specs, out_specs=[VMEM] * len(out_shap...  14.1 us
    ppermute x14, waiting for transfers between devices, body(): send = lambda value, pairs: lax.ppermute(value, 'unit', pairs)  9.64 us
  transfers between devices with their start and end apart: 14, of which 8 were waited for; matrix products, arithmetic and copies ran while one was open for 0% of the time, Pallas kernels for 36%

profile of v4, /device:TPU:0, one launch (start us, length us, event | category | flops | bytes accessed | tf_op | source)
XLA Modules:
  0.0 41.2 jit_solution(12902713847922280084)
XLA Ops:
  0.0 2.5 %collective-permute-start = (bf16[16,8192]{1,0:T(8,128)(2,1)}, bf16[16,8192]{1,0:T(8,128)(2,1)S(1)}, u32[]{:S(2)}, u32[]{:S(2)}) collective-permute-start(bf16[16,8192]{1,0:T(8,128)(2,1)} %refs_0_.2), channel_id=1, source_target_pairs={{0,5},{1,2},{4,9},{5,0},{8,13},{9,4},{12,15},{13,8},{14,11},{15,12... | collective-permute-start | bytes 786440 | tf_op jit(solution)/shard_map/ppermute | solution.py:261
  2.5 0.5 %collective-permute-start.2 = (bf16[16,8192]{1,0:T(8,128)(2,1)}, bf16[16,8192]{1,0:T(8,128)(2,1)S(1)}, u32[]{:S(2)}, u32[]{:S(2)}) collective-permute-start(bf16[16,8192]{1,0:T(8,128)(2,1)} %refs_0_.2), channel_id=1, source_target_pairs={{1,5},{0,2},{5,9},{4,0},{9,13},{8,4},{13,15},{12,8},{15,11},{14,12... | collective-permute-start | bytes 786440 | tf_op jit(solution)/shard_map/ppermute | solution.py:261
  3.0 5.8 %shard_map.37 = (bf16[256,1792]{1,0:T(8,128)(2,1)S(1)}, f32[256,1024]{1,0:T(8,128)S(1)}, bf16[3072,1792]{1,0:T(8,128)(2,1)S(1)}) custom-call(bf16[256,1792]{1,0:T(8,128)(2,1)} %x_ref.1, bf16[8192,1792]{1,0:T(8,128)(2,1)} %q_ref.7), custom_call_target="tpu_custom_call" | custom-call | flops 939524096 | bytes 3670016 | tf_op jit(solution)/shard_map/pallas_call | solution.py:136
  8.8 0.6 %collective-permute-done.refs_0_.refs_1_ = bf16[16,8192]{1,0:T(8,128)(2,1)S(1)} collective-permute-done((bf16[16,8192]{1,0:T(8,128)(2,1)}, bf16[16,8192]{1,0:T(8,128)(2,1)S(1)}, u32[]{:S(2)}, u32[]{:S(2)}) %collective-permute-start) | collective-permute-done | bytes 262176 | tf_op jit(solution)/shard_map/ppermute | solution.py:261
  9.4 1.0 %collective-permute-start.1 = (bf16[16,8192]{1,0:T(8,128)(2,1)S(1)}, bf16[16,8192]{1,0:T(8,128)(2,1)S(1)}, u32[]{:S(2)}, u32[]{:S(2)}) collective-permute-start(bf16[16,8192]{1,0:T(8,128)(2,1)S(1)} %collective-permute-done.refs_0_.refs_1_), channel_id=1, source_target_pairs={{0,3},{1,4},{4,1},{5,8},{8,5},{9,12},{12,9},{13,14},{14,13},{15,10... | collective-permute-start | bytes 786440 | tf_op jit(solution)/shard_map/ppermute | solution.py:261
  10.4 0.0 collective-permute-done.2.refs_1_.refs_2_
  10.4 1.1 %collective-permute-start.5 = (bf16[16,8192]{1,0:T(8,128)(2,1)S(1)}, bf16[16,8192]{1,0:T(8,128)(2,1)S(1)}, u32[]{:S(2)}, u32[]{:S(2)}) collective-permute-start(bf16[16,8192]{1,0:T(8,128)(2,1)S(1)} %collective-permute-done.2.refs_1_.refs_2_), channel_id=1, source_target_pairs={{0,3},{1,4},{4,1},{5,8},{8,5},{9,12},{12,9},{13,14},{14,13},{15,10... | collective-permute-start | bytes 786440 | tf_op jit(solution)/shard_map/ppermute | solution.py:261
  11.5 3.7 %shard_map.38 = (f32[256,3072]{1,0:T(8,128)S(1)}, bf16[2560,1792]{1,0:T(8,128)(2,1)S(1)}) custom-call(bf16[256,1792]{1,0:T(8,128)(2,1)S(1)} %get-tuple-element.18.x, bf16[8192,1792]{1,0:T(8,128)(2,1)} %q_ref.7, bf16[3072,1792]{1,0:T(8,128)(2,1)S(1)} %get-tuple-element.19.slab, bf16[16,8192]{1,0:T(8,128)(2,1)S(1)} %collective-permute-done.refs_0_.refs_1_, ...), custom_call_target="tpu_custom_call" | custom-call | flops 2818572288 | bytes 11010048 | tf_op jit(solution)/shard_map/pallas_call | solution.py:136
  15.2 0.0 collective-permute-done.1.refs_0_.refs_3_
  15.2 2.4 %collective-permute-start.3 = (bf16[16,8192]{1,0:T(8,128)(2,1)S(1)}, bf16[16,8192]{1,0:T(8,128)(2,1)S(1)}, u32[]{:S(2)}, u32[]{:S(2)}) collective-permute-start(bf16[16,8192]{1,0:T(8,128)(2,1)S(1)} %collective-permute-done.1.refs_0_.refs_3_), channel_id=1, source_target_pairs={{0,5},{1,2},{4,9},{5,0},{8,13},{9,4},{12,15},{13,8},{14,11},{15,12... | collective-permute-start | bytes 786440 | tf_op jit(solution)/shard_map/ppermute | solution.py:261
  17.6 0.0 copy-start
  17.6 2.8 %shard_map.39 = (f32[256,2560]{1,0:T(8,128)S(1)}, bf16[1536,1792]{1,0:T(8,128)(2,1)S(1)}) custom-call(bf16[256,1792]{1,0:T(8,128)(2,1)S(1)} %get-tuple-element.18.x, bf16[8192,1792]{1,0:T(8,128)(2,1)} %q_ref.7, bf16[2560,1792]{1,0:T(8,128)(2,1)S(1)} %get-tuple-element.22.slab, bf16[16,8192]{1,0:T(8,128)(2,1)S(1)} %collective-permute-done.1.refs_0_.refs_3_), custom_call_target="tpu_custom_call" | custom-call | flops 2348810240 | bytes 9175040 | tf_op jit(solution)/shard_map/pallas_call | solution.py:136
  20.4 0.0 collective-permute-done.5.refs_4_
  20.5 0.3 collective-permute-start.6
  20.8 0.9 %collective-permute-done.3.refs_0_.refs_5_ = bf16[16,8192]{1,0:T(8,128)(2,1)S(1)} collective-permute-done((bf16[16,8192]{1,0:T(8,128)(2,1)S(1)}, bf16[16,8192]{1,0:T(8,128)(2,1)S(1)}, u32[]{:S(2)}, u32[]{:S(2)}) %collective-permute-start.3) | collective-permute-done | bytes 262176 | tf_op jit(solution)/shard_map/ppermute | solution.py:261
  21.7 0.9 %collective-permute-start.4 = (bf16[16,8192]{1,0:T(8,128)(2,1)S(1)}, bf16[16,8192]{1,0:T(8,128)(2,1)S(1)}, u32[]{:S(2)}, u32[]{:S(2)}) collective-permute-start(bf16[16,8192]{1,0:T(8,128)(2,1)S(1)} %collective-permute-done.3.refs_0_.refs_5_), channel_id=1, source_target_pairs={{0,3},{1,4},{4,1},{5,8},{8,5},{9,12},{12,9},{13,14},{14,13},{15,10... | collective-permute-start | bytes 786440 | tf_op jit(solution)/shard_map/ppermute | solution.py:261
  22.5 0.0 copy-done
  22.6 0.1 shard_map.43
  22.6 1.2 %collective-permute-start.7 = (bf16[80,8192]{1,0:T(8,128)(2,1)S(1)}, bf16[80,8192]{1,0:T(8,128)(2,1)S(1)}, u32[]{:S(2)}, u32[]{:S(2)}) collective-permute-start(bf16[80,8192]{1,0:T(8,128)(2,1)S(1)} %shard_map.43), channel_id=1, source_target_pairs={{0,1},{1,0},{4,5},{5,4},{8,9},{9,8},{12,13},{13,12},{14,15},{15,14... | collective-permute-start | bytes 3932168 | tf_op jit(solution)/shard_map/ppermute | solution.py:261
  23.8 1.8 %shard_map.40.refs_10_.refs_3_.refs_9_ = f32[256,1536]{1,0:T(8,128)S(1)} custom-call(bf16[256,1792]{1,0:T(8,128)(2,1)S(1)} %get-tuple-element.18.x, bf16[8192,1792]{1,0:T(8,128)(2,1)} %q_ref.7, bf16[1536,1792]{1,0:T(8,128)(2,1)S(1)} %get-tuple-element.25.slab, bf16[16,8192]{1,0:T(8,128)(2,1)S(1)} %collective-permute-done.3.refs_0_.refs_5_), custom_call_target="tpu_custom_call" | custom-call | flops 1409286144 | bytes 5505024 | tf_op jit(solution)/shard_map/pallas_call | solution.py:136
  25.6 0.1 shard_map.44
  25.7 0.1 collective-permute-start.9
  25.8 0.5 %collective-permute-start.8 = (bf16[16,8192]{1,0:T(8,128)(2,1)S(1)}, bf16[16,8192]{1,0:T(8,128)(2,1)S(1)}, u32[]{:S(2)}, u32[]{:S(2)}) collective-permute-start(bf16[16,8192]{1,0:T(8,128)(2,1)S(1)} %collective-permute-done.3.refs_0_.refs_5_), channel_id=1, source_target_pairs={{0,1},{1,0},{4,5},{5,4},{8,9},{9,8},{12,13},{13,12},{14,15},{15,14... | collective-permute-start | bytes 786440 | tf_op jit(solution)/shard_map/ppermute | solution.py:261
  26.3 1.2 %collective-permute-done.6.refs_6_.refs_0_ = bf16[16,8192]{1,0:T(8,128)(2,1)S(1)} collective-permute-done((bf16[16,8192]{1,0:T(8,128)(2,1)S(1)}, bf16[16,8192]{1,0:T(8,128)(2,1)S(1)}, u32[]{:S(2)}, u32[]{:S(2)}) %collective-permute-start.6) | collective-permute-done | bytes 262176 | tf_op jit(solution)/shard_map/ppermute | solution.py:261
  27.5 0.5 %shard_map.41.table.refs_5_ = f32[256,128]{1,0:T(8,128)S(1)} custom-call(bf16[16,8192]{1,0:T(8,128)(2,1)S(1)} %copy-done, bf16[16,8192]{1,0:T(8,128)(2,1)S(1)} %collective-permute-done.refs_0_.refs_1_, bf16[16,8192]{1,0:T(8,128)(2,1)S(1)} %collective-permute-done.2.refs_1_.refs_2_, bf16[16,8192]{1,0:T(8,128)(2,1)S(1)} %collective-permute-done.1.refs_0_.refs_3_, ...), custom_call_target="tpu_custom_call" | custom-call | tf_op jit(solution)/shard_map/pallas_call | solution.py:202
  28.0 0.9 %collective-permute-done.4.last.refs_1_ = bf16[16,8192]{1,0:T(8,128)(2,1)S(1)} collective-permute-done((bf16[16,8192]{1,0:T(8,128)(2,1)S(1)}, bf16[16,8192]{1,0:T(8,128)(2,1)S(1)}, u32[]{:S(2)}, u32[]{:S(2)}) %collective-permute-start.4) | collective-permute-done | bytes 262176 | tf_op jit(solution)/shard_map/ppermute | solution.py:261
  28.8 0.0 collective-permute-done.8.refs_3_
  28.8 0.0 collective-permute-done.9.refs_4_
  28.8 0.0 collective-permute-done.7.refs_2_
  28.9 0.6 %shard_map.45 = f32[1,256]{1,0:T(1,128)S(1)} custom-call(f32[8,128]{1,0:T(8,128)S(1)} %shard_map.42.arrived, bf16[16,8192]{1,0:T(8,128)(2,1)S(1)} %collective-permute-done.6.refs_6_.refs_0_, bf16[16,8192]{1,0:T(8,128)(2,1)S(1)} %collective-permute-done.4.last.refs_1_, bf16[80,8192]{1,0:T(8,128)(2,1)S(1)} %collective-permute-done.7.refs_2_, ...), custom_call_target="tpu_custom_call" | custom-call | tf_op jit(solution)/shard_map/pallas_call | solution.py:324
  29.5 0.2 collective-permute-start.10
  29.7 1.0 %collective-permute-done.10 = f32[1,256]{1,0:T(1,128)S(1)} collective-permute-done((f32[1,256]{1,0:T(1,128)S(1)}, f32[1,256]{1,0:T(1,128)S(1)}, u32[]{:S(2)}, u32[]{:S(2)}) %collective-permute-start.10) | collective-permute-done | bytes 1056 | tf_op jit(solution)/shard_map/ppermute | solution.py:261
  30.7 1.4 %collective-permute-start.11 = (f32[1,256]{1,0:T(1,128)S(1)}, f32[1,256]{1,0:T(1,128)S(1)}, u32[]{:S(2)}, u32[]{:S(2)}) collective-permute-start(f32[1,256]{1,0:T(1,128)S(1)} %add.12), channel_id=1, source_target_pairs={{0,3},{1,2},{2,1},{3,0},{4,7},{5,6},{6,5},{7,4},{8,11},{9,10},{10,... | collective-permute-start | bytes 3080 | tf_op jit(solution)/shard_map/ppermute | solution.py:261
  32.1 1.6 %collective-permute-done.11 = f32[1,256]{1,0:T(1,128)S(1)} collective-permute-done((f32[1,256]{1,0:T(1,128)S(1)}, f32[1,256]{1,0:T(1,128)S(1)}, u32[]{:S(2)}, u32[]{:S(2)}) %collective-permute-start.11) | collective-permute-done | bytes 1056 | tf_op jit(solution)/shard_map/ppermute | solution.py:261
  33.7 1.2 %collective-permute-start.12 = (f32[1,256]{1,0:T(1,128)S(1)}, f32[1,256]{1,0:T(1,128)S(1)}, u32[]{:S(2)}, u32[]{:S(2)}) collective-permute-start(f32[1,256]{1,0:T(1,128)S(1)} %add.13), channel_id=1, source_target_pairs={{0,5},{1,4},{2,7},{3,6},{4,1},{5,0},{6,3},{7,2},{8,13},{9,12},{10,... | collective-permute-start | bytes 3080 | tf_op jit(solution)/shard_map/ppermute | solution.py:261
  34.9 1.7 %collective-permute-done.12 = f32[1,256]{1,0:T(1,128)S(1)} collective-permute-done((f32[1,256]{1,0:T(1,128)S(1)}, f32[1,256]{1,0:T(1,128)S(1)}, u32[]{:S(2)}, u32[]{:S(2)}) %collective-permute-start.12) | collective-permute-done | bytes 1056 | tf_op jit(solution)/shard_map/ppermute | solution.py:261
  36.7 2.3 %collective-permute-start.13 = (f32[1,256]{1,0:T(1,128)S(1)}, f32[1,256]{1,0:T(1,128)S(1)}, u32[]{:S(2)}, u32[]{:S(2)}) collective-permute-start(f32[1,256]{1,0:T(1,128)S(1)} %add.14), channel_id=1, source_target_pairs={{0,9},{1,8},{2,11},{3,10},{4,13},{5,12},{6,15},{7,14},{8,1},{9,0},... | collective-permute-start | bytes 3080 | tf_op jit(solution)/shard_map/ppermute | solution.py:261
  39.0 1.6 %collective-permute-done.13 = f32[1,256]{1,0:T(1,128)S(1)} collective-permute-done((f32[1,256]{1,0:T(1,128)S(1)}, f32[1,256]{1,0:T(1,128)S(1)}, u32[]{:S(2)}, u32[]{:S(2)}) %collective-permute-start.13) | collective-permute-done | bytes 1056 | tf_op jit(solution)/shard_map/ppermute | solution.py:261
  40.6 0.6 %add.15 = f32[1,256]{1,0:T(1,128)} add(f32[1,256]{1,0:T(1,128)S(1)} %add.14, f32[1,256]{1,0:T(1,128)S(1)} %collective-permute-done.13) | non-fusion elementwise | flops 256 | bytes 3072 | tf_op jit(solution)/shard_map/add | solution.py:336
  (4 shorter events, 0.0 us)
Async XLA Ops:
  0.0 9.4 %collective-permute-start = (bf16[16,8192]{1,0:T(8,128)(2,1)}, bf16[16,8192]{1,0:T(8,128)(2,1)S(1)}, u32[]{:S(2)}, u32[]{:S(2)}) collective-permute-start(bf16[16,8192]{1,0:T(8,128)(2,1)} %refs_0_.2), channel_id=1, source_target_pairs={{0,5},{1,2},{4,9},{5,0},{8,13},{9,4},{12,15},{13,8},{14,11},{15,12... | collective-permute-start | bytes 786440 | tf_op jit(solution)/shard_map/ppermute | solution.py:261
  2.5 8.0 %collective-permute-start.2 = (bf16[16,8192]{1,0:T(8,128)(2,1)}, bf16[16,8192]{1,0:T(8,128)(2,1)S(1)}, u32[]{:S(2)}, u32[]{:S(2)}) collective-permute-start(bf16[16,8192]{1,0:T(8,128)(2,1)} %refs_0_.2), channel_id=1, source_target_pairs={{1,5},{0,2},{5,9},{4,0},{9,13},{8,4},{13,15},{12,8},{15,11},{14,12... | collective-permute-start | bytes 786440 | tf_op jit(solution)/shard_map/ppermute | solution.py:261
  9.4 5.8 %collective-permute-start.1 = (bf16[16,8192]{1,0:T(8,128)(2,1)S(1)}, bf16[16,8192]{1,0:T(8,128)(2,1)S(1)}, u32[]{:S(2)}, u32[]{:S(2)}) collective-permute-start(bf16[16,8192]{1,0:T(8,128)(2,1)S(1)} %collective-permute-done.refs_0_.refs_1_), channel_id=1, source_target_pairs={{0,3},{1,4},{4,1},{5,8},{8,5},{9,12},{12,9},{13,14},{14,13},{15,10... | collective-permute-start | bytes 786440 | tf_op jit(solution)/shard_map/ppermute | solution.py:261
  10.4 10.0 %collective-permute-start.5 = (bf16[16,8192]{1,0:T(8,128)(2,1)S(1)}, bf16[16,8192]{1,0:T(8,128)(2,1)S(1)}, u32[]{:S(2)}, u32[]{:S(2)}) collective-permute-start(bf16[16,8192]{1,0:T(8,128)(2,1)S(1)} %collective-permute-done.2.refs_1_.refs_2_), channel_id=1, source_target_pairs={{0,3},{1,4},{4,1},{5,8},{8,5},{9,12},{12,9},{13,14},{14,13},{15,10... | collective-permute-start | bytes 786440 | tf_op jit(solution)/shard_map/ppermute | solution.py:261
  15.2 6.4 %collective-permute-start.3 = (bf16[16,8192]{1,0:T(8,128)(2,1)S(1)}, bf16[16,8192]{1,0:T(8,128)(2,1)S(1)}, u32[]{:S(2)}, u32[]{:S(2)}) collective-permute-start(bf16[16,8192]{1,0:T(8,128)(2,1)S(1)} %collective-permute-done.1.refs_0_.refs_3_), channel_id=1, source_target_pairs={{0,5},{1,2},{4,9},{5,0},{8,13},{9,4},{12,15},{13,8},{14,11},{15,12... | collective-permute-start | bytes 786440 | tf_op jit(solution)/shard_map/ppermute | solution.py:261
  17.6 4.9 %copy-start = (bf16[16,8192]{1,0:T(8,128)(2,1)S(1)}, bf16[16,8192]{1,0:T(8,128)(2,1)}, u32[]{:S(2)}) copy-start(bf16[16,8192]{1,0:T(8,128)(2,1)} %refs_0_.2) | copy-start | bytes 786436
  20.5 7.0 %collective-permute-start.6 = (bf16[16,8192]{1,0:T(8,128)(2,1)S(1)}, bf16[16,8192]{1,0:T(8,128)(2,1)S(1)}, u32[]{:S(2)}, u32[]{:S(2)}) collective-permute-start(bf16[16,8192]{1,0:T(8,128)(2,1)S(1)} %collective-permute-done.5.refs_4_), channel_id=1, source_target_pairs={{0,5},{1,2},{4,9},{5,0},{8,13},{9,4},{12,15},{13,8},{14,11},{15,12... | collective-permute-start | bytes 786440 | tf_op jit(solution)/shard_map/ppermute | solution.py:261
  21.7 7.1 %collective-permute-start.4 = (bf16[16,8192]{1,0:T(8,128)(2,1)S(1)}, bf16[16,8192]{1,0:T(8,128)(2,1)S(1)}, u32[]{:S(2)}, u32[]{:S(2)}) collective-permute-start(bf16[16,8192]{1,0:T(8,128)(2,1)S(1)} %collective-permute-done.3.refs_0_.refs_5_), channel_id=1, source_target_pairs={{0,3},{1,4},{4,1},{5,8},{8,5},{9,12},{12,9},{13,14},{14,13},{15,10... | collective-permute-start | bytes 786440 | tf_op jit(solution)/shard_map/ppermute | solution.py:261
  22.6 6.2 %collective-permute-start.7 = (bf16[80,8192]{1,0:T(8,128)(2,1)S(1)}, bf16[80,8192]{1,0:T(8,128)(2,1)S(1)}, u32[]{:S(2)}, u32[]{:S(2)}) collective-permute-start(bf16[80,8192]{1,0:T(8,128)(2,1)S(1)} %shard_map.43), channel_id=1, source_target_pairs={{0,1},{1,0},{4,5},{5,4},{8,9},{9,8},{12,13},{13,12},{14,15},{15,14... | collective-permute-start | bytes 3932168 | tf_op jit(solution)/shard_map/ppermute | solution.py:261
  25.7 3.1 %collective-permute-start.9 = (f32[32,8192]{1,0:T(8,128)S(1)}, f32[32,8192]{1,0:T(8,128)S(1)}, u32[]{:S(2)}, u32[]{:S(2)}) collective-permute-start(f32[32,8192]{1,0:T(8,128)S(1)} %shard_map.44), channel_id=1, source_target_pairs={{0,1},{1,0},{4,5},{5,4},{8,9},{9,8},{12,13},{13,12},{14,15},{15,14... | collective-permute-start | bytes 3145736 | tf_op jit(solution)/shard_map/ppermute | solution.py:261
  25.8 3.0 %collective-permute-start.8 = (bf16[16,8192]{1,0:T(8,128)(2,1)S(1)}, bf16[16,8192]{1,0:T(8,128)(2,1)S(1)}, u32[]{:S(2)}, u32[]{:S(2)}) collective-permute-start(bf16[16,8192]{1,0:T(8,128)(2,1)S(1)} %collective-permute-done.3.refs_0_.refs_5_), channel_id=1, source_target_pairs={{0,1},{1,0},{4,5},{5,4},{8,9},{9,8},{12,13},{13,12},{14,15},{15,14... | collective-permute-start | bytes 786440 | tf_op jit(solution)/shard_map/ppermute | solution.py:261
  29.5 1.2 %collective-permute-start.10 = (f32[1,256]{1,0:T(1,128)S(1)}, f32[1,256]{1,0:T(1,128)S(1)}, u32[]{:S(2)}, u32[]{:S(2)}) collective-permute-start(f32[1,256]{1,0:T(1,128)S(1)} %shard_map.45), channel_id=1, source_target_pairs={{0,1},{1,0},{2,3},{3,2},{4,5},{5,4},{6,7},{7,6},{8,9},{9,8},{10,11... | collective-permute-start | bytes 3080 | tf_op jit(solution)/shard_map/ppermute | solution.py:261
  30.7 3.0 %collective-permute-start.11 = (f32[1,256]{1,0:T(1,128)S(1)}, f32[1,256]{1,0:T(1,128)S(1)}, u32[]{:S(2)}, u32[]{:S(2)}) collective-permute-start(f32[1,256]{1,0:T(1,128)S(1)} %add.12), channel_id=1, source_target_pairs={{0,3},{1,2},{2,1},{3,0},{4,7},{5,6},{6,5},{7,4},{8,11},{9,10},{10,... | collective-permute-start | bytes 3080 | tf_op jit(solution)/shard_map/ppermute | solution.py:261
  33.7 3.0 %collective-permute-start.12 = (f32[1,256]{1,0:T(1,128)S(1)}, f32[1,256]{1,0:T(1,128)S(1)}, u32[]{:S(2)}, u32[]{:S(2)}) collective-permute-start(f32[1,256]{1,0:T(1,128)S(1)} %add.13), channel_id=1, source_target_pairs={{0,5},{1,4},{2,7},{3,6},{4,1},{5,0},{6,3},{7,2},{8,13},{9,12},{10,... | collective-permute-start | bytes 3080 | tf_op jit(solution)/shard_map/ppermute | solution.py:261
  36.7 3.9 %collective-permute-start.13 = (f32[1,256]{1,0:T(1,128)S(1)}, f32[1,256]{1,0:T(1,128)S(1)}, u32[]{:S(2)}, u32[]{:S(2)}) collective-permute-start(f32[1,256]{1,0:T(1,128)S(1)} %add.14), channel_id=1, source_target_pairs={{0,9},{1,8},{2,11},{3,10},{4,13},{5,12},{6,15},{7,14},{8,1},{9,0},... | collective-permute-start | bytes 3080 | tf_op jit(solution)/shard_map/ppermute | solution.py:261

commit v5 on v4

--- a/solution.py
+++ b/solution.py
@@ -330,10 +330,15 @@
         compiler_params=pltpu.CompilerParams(vmem_limit_bytes=GRANT),
     )(arrived, held[-1], last, given, more, theirs, table, *weights)
 
-    bit = 1
+    def moved(bits):
+        return send(partial_value, [(unit, unit ^ bits) for unit in range(units)])
+
+    partial_value += moved(1)
+    far, both, near = moved(5), moved(7), moved(3)
+    partial_value = (partial_value + far) + (both + near)
+    bit = 8
     while bit < units:
-        pairs = [(unit, unit ^ bit ^ (bit > 1)) for unit in range(units)]
-        partial_value += send(partial_value, pairs)
+        partial_value += moved(bit + 1)
         bit *= 2
     return partial_value.reshape(tokens)
 

time: 41.3 us -> 41.1 us (level)
  waiting for transfers between devices: 9.64 us -> 8.72 us
  starting transfers between devices: 15.4 us -> 16.1 us
    ppermute x14 -> x15, waiting for transfers between devices: 9.64 us -> 8.72 us  [body(): send = lambda value, pairs: lax.ppermute(value, 'unit', pairs)]
    ppermute x14 -> x15, starting transfers between devices: 15.4 us -> 16.1 us  [body(): send = lambda value, pairs: lax.ppermute(value, 'unit', pairs)]
  transfers between devices with their start and end apart: 14 -> 15, of which waited for: 8 -> 8; matrix products, arithmetic and copies ran while one was open for 0% -> 0% of each run, Pallas kernels for 36% -> 36%
where the time goes in v5:
time: 41.1 us; the launch traced here: 40.9 us
  starting transfers between devices  16.1 us (39%)
  Pallas kernels  15.4 us (37%)
  waiting for transfers between devices  8.72 us (21%)
  other arithmetic  0.57 us (1%)
    ppermute x15, starting transfers between devices, body(): send = lambda value, pairs: lax.ppermute(value, 'unit', pairs)  16.1 us
    pallas_call x4, Pallas kernels, weigh(): pl.pallas_call(kernel, in_specs=in_specs, out_specs=[VMEM] * len(out_shap...  14.1 us
    ppermute x15, waiting for transfers between devices, body(): send = lambda value, pairs: lax.ppermute(value, 'unit', pairs)  8.72 us
  transfers between devices with their start and end apart: 15, of which 8 were waited for; matrix products, arithmetic and copies ran while one was open for 0% of the time, Pallas kernels for 36%

profile of v5, /device:TPU:0, one launch (start us, length us, event | category | flops | bytes accessed | tf_op | source)
XLA Modules:
  0.0 40.9 jit_solution(1839839705443130128)
XLA Ops:
  0.0 2.5 %collective-permute-start = (bf16[16,8192]{1,0:T(8,128)(2,1)}, bf16[16,8192]{1,0:T(8,128)(2,1)S(1)}, u32[]{:S(2)}, u32[]{:S(2)}) collective-permute-start(bf16[16,8192]{1,0:T(8,128)(2,1)} %refs_0_.2), channel_id=1, source_target_pairs={{0,5},{1,2},{4,9},{5,0},{8,13},{9,4},{12,15},{13,8},{14,11},{15,12... | collective-permute-start | bytes 786440 | tf_op jit(solution)/shard_map/ppermute | solution.py:261
  2.5 0.5 %collective-permute-start.2 = (bf16[16,8192]{1,0:T(8,128)(2,1)}, bf16[16,8192]{1,0:T(8,128)(2,1)S(1)}, u32[]{:S(2)}, u32[]{:S(2)}) collective-permute-start(bf16[16,8192]{1,0:T(8,128)(2,1)} %refs_0_.2), channel_id=1, source_target_pairs={{1,5},{0,2},{5,9},{4,0},{9,13},{8,4},{13,15},{12,8},{15,11},{14,12... | collective-permute-start | bytes 786440 | tf_op jit(solution)/shard_map/ppermute | solution.py:261
  3.0 5.8 %shard_map.37 = (bf16[256,1792]{1,0:T(8,128)(2,1)S(1)}, f32[256,1024]{1,0:T(8,128)S(1)}, bf16[3072,1792]{1,0:T(8,128)(2,1)S(1)}) custom-call(bf16[256,1792]{1,0:T(8,128)(2,1)} %x_ref.1, bf16[8192,1792]{1,0:T(8,128)(2,1)} %q_ref.7), custom_call_target="tpu_custom_call" | custom-call | flops 939524096 | bytes 3670016 | tf_op jit(solution)/shard_map/pallas_call | solution.py:136
  8.8 0.6 %collective-permute-done.refs_0_.refs_1_ = bf16[16,8192]{1,0:T(8,128)(2,1)S(1)} collective-permute-done((bf16[16,8192]{1,0:T(8,128)(2,1)}, bf16[16,8192]{1,0:T(8,128)(2,1)S(1)}, u32[]{:S(2)}, u32[]{:S(2)}) %collective-permute-start) | collective-permute-done | bytes 262176 | tf_op jit(solution)/shard_map/ppermute | solution.py:261
  9.4 1.0 %collective-permute-start.1 = (bf16[16,8192]{1,0:T(8,128)(2,1)S(1)}, bf16[16,8192]{1,0:T(8,128)(2,1)S(1)}, u32[]{:S(2)}, u32[]{:S(2)}) collective-permute-start(bf16[16,8192]{1,0:T(8,128)(2,1)S(1)} %collective-permute-done.refs_0_.refs_1_), channel_id=1, source_target_pairs={{0,3},{1,4},{4,1},{5,8},{8,5},{9,12},{12,9},{13,14},{14,13},{15,10... | collective-permute-start | bytes 786440 | tf_op jit(solution)/shard_map/ppermute | solution.py:261
  10.4 0.0 collective-permute-done.2.refs_1_.refs_2_
  10.4 1.1 %collective-permute-start.5 = (bf16[16,8192]{1,0:T(8,128)(2,1)S(1)}, bf16[16,8192]{1,0:T(8,128)(2,1)S(1)}, u32[]{:S(2)}, u32[]{:S(2)}) collective-permute-start(bf16[16,8192]{1,0:T(8,128)(2,1)S(1)} %collective-permute-done.2.refs_1_.refs_2_), channel_id=1, source_target_pairs={{0,3},{1,4},{4,1},{5,8},{8,5},{9,12},{12,9},{13,14},{14,13},{15,10... | collective-permute-start | bytes 786440 | tf_op jit(solution)/shard_map/ppermute | solution.py:261
  11.5 3.7 %shard_map.38 = (f32[256,3072]{1,0:T(8,128)S(1)}, bf16[2560,1792]{1,0:T(8,128)(2,1)S(1)}) custom-call(bf16[256,1792]{1,0:T(8,128)(2,1)S(1)} %get-tuple-element.18.x, bf16[8192,1792]{1,0:T(8,128)(2,1)} %q_ref.7, bf16[3072,1792]{1,0:T(8,128)(2,1)S(1)} %get-tuple-element.19.slab, bf16[16,8192]{1,0:T(8,128)(2,1)S(1)} %collective-permute-done.refs_0_.refs_1_, ...), custom_call_target="tpu_custom_call" | custom-call | flops 2818572288 | bytes 11010048 | tf_op jit(solution)/shard_map/pallas_call | solution.py:136
  15.2 0.0 collective-permute-done.1.refs_0_.refs_3_
  15.2 2.4 %collective-permute-start.3 = (bf16[16,8192]{1,0:T(8,128)(2,1)S(1)}, bf16[16,8192]{1,0:T(8,128)(2,1)S(1)}, u32[]{:S(2)}, u32[]{:S(2)}) collective-permute-start(bf16[16,8192]{1,0:T(8,128)(2,1)S(1)} %collective-permute-done.1.refs_0_.refs_3_), channel_id=1, source_target_pairs={{0,5},{1,2},{4,9},{5,0},{8,13},{9,4},{12,15},{13,8},{14,11},{15,12... | collective-permute-start | bytes 786440 | tf_op jit(solution)/shard_map/ppermute | solution.py:261
  17.6 0.0 copy-start
  17.6 2.8 %shard_map.39 = (f32[256,2560]{1,0:T(8,128)S(1)}, bf16[1536,1792]{1,0:T(8,128)(2,1)S(1)}) custom-call(bf16[256,1792]{1,0:T(8,128)(2,1)S(1)} %get-tuple-element.18.x, bf16[8192,1792]{1,0:T(8,128)(2,1)} %q_ref.7, bf16[2560,1792]{1,0:T(8,128)(2,1)S(1)} %get-tuple-element.22.slab, bf16[16,8192]{1,0:T(8,128)(2,1)S(1)} %collective-permute-done.1.refs_0_.refs_3_), custom_call_target="tpu_custom_call" | custom-call | flops 2348810240 | bytes 9175040 | tf_op jit(solution)/shard_map/pallas_call | solution.py:136
  20.4 0.0 collective-permute-done.5.refs_4_
  20.5 0.3 collective-permute-start.6
  20.8 0.9 %collective-permute-done.3.refs_0_.refs_5_ = bf16[16,8192]{1,0:T(8,128)(2,1)S(1)} collective-permute-done((bf16[16,8192]{1,0:T(8,128)(2,1)S(1)}, bf16[16,8192]{1,0:T(8,128)(2,1)S(1)}, u32[]{:S(2)}, u32[]{:S(2)}) %collective-permute-start.3) | collective-permute-done | bytes 262176 | tf_op jit(solution)/shard_map/ppermute | solution.py:261
  21.7 0.9 %collective-permute-start.4 = (bf16[16,8192]{1,0:T(8,128)(2,1)S(1)}, bf16[16,8192]{1,0:T(8,128)(2,1)S(1)}, u32[]{:S(2)}, u32[]{:S(2)}) collective-permute-start(bf16[16,8192]{1,0:T(8,128)(2,1)S(1)} %collective-permute-done.3.refs_0_.refs_5_), channel_id=1, source_target_pairs={{0,3},{1,4},{4,1},{5,8},{8,5},{9,12},{12,9},{13,14},{14,13},{15,10... | collective-permute-start | bytes 786440 | tf_op jit(solution)/shard_map/ppermute | solution.py:261
  22.5 0.0 copy-done
  22.6 0.1 shard_map.43
  22.6 1.2 %collective-permute-start.7 = (bf16[80,8192]{1,0:T(8,128)(2,1)S(1)}, bf16[80,8192]{1,0:T(8,128)(2,1)S(1)}, u32[]{:S(2)}, u32[]{:S(2)}) collective-permute-start(bf16[80,8192]{1,0:T(8,128)(2,1)S(1)} %shard_map.43), channel_id=1, source_target_pairs={{0,1},{1,0},{4,5},{5,4},{8,9},{9,8},{12,13},{13,12},{14,15},{15,14... | collective-permute-start | bytes 3932168 | tf_op jit(solution)/shard_map/ppermute | solution.py:261
  23.8 1.8 %shard_map.40.refs_10_.refs_3_.refs_9_ = f32[256,1536]{1,0:T(8,128)S(1)} custom-call(bf16[256,1792]{1,0:T(8,128)(2,1)S(1)} %get-tuple-element.18.x, bf16[8192,1792]{1,0:T(8,128)(2,1)} %q_ref.7, bf16[1536,1792]{1,0:T(8,128)(2,1)S(1)} %get-tuple-element.25.slab, bf16[16,8192]{1,0:T(8,128)(2,1)S(1)} %collective-permute-done.3.refs_0_.refs_5_), custom_call_target="tpu_custom_call" | custom-call | flops 1409286144 | bytes 5505024 | tf_op jit(solution)/shard_map/pallas_call | solution.py:136
  25.6 0.1 shard_map.44
  25.7 0.1 collective-permute-start.9
  25.8 0.5 %collective-permute-start.8 = (bf16[16,8192]{1,0:T(8,128)(2,1)S(1)}, bf16[16,8192]{1,0:T(8,128)(2,1)S(1)}, u32[]{:S(2)}, u32[]{:S(2)}) collective-permute-start(bf16[16,8192]{1,0:T(8,128)(2,1)S(1)} %collective-permute-done.3.refs_0_.refs_5_), channel_id=1, source_target_pairs={{0,1},{1,0},{4,5},{5,4},{8,9},{9,8},{12,13},{13,12},{14,15},{15,14... | collective-permute-start | bytes 786440 | tf_op jit(solution)/shard_map/ppermute | solution.py:261
  26.3 1.2 %collective-permute-done.6.refs_6_.refs_0_ = bf16[16,8192]{1,0:T(8,128)(2,1)S(1)} collective-permute-done((bf16[16,8192]{1,0:T(8,128)(2,1)S(1)}, bf16[16,8192]{1,0:T(8,128)(2,1)S(1)}, u32[]{:S(2)}, u32[]{:S(2)}) %collective-permute-start.6) | collective-permute-done | bytes 262176 | tf_op jit(solution)/shard_map/ppermute | solution.py:261
  27.5 0.5 %shard_map.41.table.refs_5_ = f32[256,128]{1,0:T(8,128)S(1)} custom-call(bf16[16,8192]{1,0:T(8,128)(2,1)S(1)} %copy-done, bf16[16,8192]{1,0:T(8,128)(2,1)S(1)} %collective-permute-done.refs_0_.refs_1_, bf16[16,8192]{1,0:T(8,128)(2,1)S(1)} %collective-permute-done.2.refs_1_.refs_2_, bf16[16,8192]{1,0:T(8,128)(2,1)S(1)} %collective-permute-done.1.refs_0_.refs_3_, ...), custom_call_target="tpu_custom_call" | custom-call | tf_op jit(solution)/shard_map/pallas_call | solution.py:202
  28.0 0.9 %collective-permute-done.4.last.refs_1_ = bf16[16,8192]{1,0:T(8,128)(2,1)S(1)} collective-permute-done((bf16[16,8192]{1,0:T(8,128)(2,1)S(1)}, bf16[16,8192]{1,0:T(8,128)(2,1)S(1)}, u32[]{:S(2)}, u32[]{:S(2)}) %collective-permute-start.4) | collective-permute-done | bytes 262176 | tf_op jit(solution)/shard_map/ppermute | solution.py:261
  28.8 0.0 collective-permute-done.8.refs_3_
  28.8 0.0 collective-permute-done.9.refs_4_
  28.8 0.0 collective-permute-done.7.refs_2_
  28.9 0.6 %shard_map.45 = f32[1,256]{1,0:T(1,128)S(1)} custom-call(f32[8,128]{1,0:T(8,128)S(1)} %shard_map.42.arrived, bf16[16,8192]{1,0:T(8,128)(2,1)S(1)} %collective-permute-done.6.refs_6_.refs_0_, bf16[16,8192]{1,0:T(8,128)(2,1)S(1)} %collective-permute-done.4.last.refs_1_, bf16[80,8192]{1,0:T(8,128)(2,1)S(1)} %collective-permute-done.7.refs_2_, ...), custom_call_target="tpu_custom_call" | custom-call | tf_op jit(solution)/shard_map/pallas_call | solution.py:324
  29.5 0.2 collective-permute-start.10
  29.7 1.0 %collective-permute-done.10 = f32[1,256]{1,0:T(1,128)S(1)} collective-permute-done((f32[1,256]{1,0:T(1,128)S(1)}, f32[1,256]{1,0:T(1,128)S(1)}, u32[]{:S(2)}, u32[]{:S(2)}) %collective-permute-start.10) | collective-permute-done | bytes 1056 | tf_op jit(solution)/shard_map/ppermute | solution.py:261
  30.7 1.2 %collective-permute-start.11 = (f32[1,256]{1,0:T(1,128)S(1)}, f32[1,256]{1,0:T(1,128)S(1)}, u32[]{:S(2)}, u32[]{:S(2)}) collective-permute-start(f32[1,256]{1,0:T(1,128)S(1)} %add.15), channel_id=1, source_target_pairs={{0,5},{1,4},{2,7},{3,6},{4,1},{5,0},{6,3},{7,2},{8,13},{9,12},{10,... | collective-permute-start | bytes 3080 | tf_op jit(solution)/shard_map/ppermute | solution.py:261
  31.9 1.5 %collective-permute-start.12 = (f32[1,256]{1,0:T(1,128)S(1)}, f32[1,256]{1,0:T(1,128)S(1)}, u32[]{:S(2)}, u32[]{:S(2)}) collective-permute-start(f32[1,256]{1,0:T(1,128)S(1)} %add.15), channel_id=1, source_target_pairs={{0,7},{1,6},{2,5},{3,4},{4,3},{5,2},{6,1},{7,0},{8,15},{9,14},{10,... | collective-permute-start | bytes 3080 | tf_op jit(solution)/shard_map/ppermute | solution.py:261
  33.5 0.2 collective-permute-start.13
  33.7 0.0 collective-permute-done.11
  33.7 2.1 %collective-permute-done.12 = f32[1,256]{1,0:T(1,128)S(1)} collective-permute-done((f32[1,256]{1,0:T(1,128)S(1)}, f32[1,256]{1,0:T(1,128)S(1)}, u32[]{:S(2)}, u32[]{:S(2)}) %collective-permute-start.12) | collective-permute-done | bytes 1056 | tf_op jit(solution)/shard_map/ppermute | solution.py:261
  35.8 0.6 %collective-permute-done.13 = f32[1,256]{1,0:T(1,128)S(1)} collective-permute-done((f32[1,256]{1,0:T(1,128)S(1)}, f32[1,256]{1,0:T(1,128)S(1)}, u32[]{:S(2)}, u32[]{:S(2)}) %collective-permute-start.13) | collective-permute-done | bytes 1056 | tf_op jit(solution)/shard_map/ppermute | solution.py:261
  36.5 2.6 %collective-permute-start.14 = (f32[1,256]{1,0:T(1,128)S(1)}, f32[1,256]{1,0:T(1,128)S(1)}, u32[]{:S(2)}, u32[]{:S(2)}) collective-permute-start(f32[1,256]{1,0:T(1,128)S(1)} %add_add_fusion), channel_id=1, source_target_pairs={{0,9},{1,8},{2,11},{3,10},{4,13},{5,12},{6,15},{7,14},{8,1},{9,0},... | collective-permute-start | bytes 3080 | tf_op jit(solution)/shard_map/ppermute | solution.py:261
  39.0 1.3 %collective-permute-done.14 = f32[1,256]{1,0:T(1,128)S(1)} collective-permute-done((f32[1,256]{1,0:T(1,128)S(1)}, f32[1,256]{1,0:T(1,128)S(1)}, u32[]{:S(2)}, u32[]{:S(2)}) %collective-permute-start.14) | collective-permute-done | bytes 1056 | tf_op jit(solution)/shard_map/ppermute | solution.py:261
  40.3 0.6 %add.19 = f32[1,256]{1,0:T(1,128)} add(f32[1,256]{1,0:T(1,128)S(1)} %add_add_fusion, f32[1,256]{1,0:T(1,128)S(1)} %collective-permute-done.14) | non-fusion elementwise | flops 256 | bytes 3072 | tf_op jit(solution)/shard_map/add | solution.py:341
  (3 shorter events, 0.0 us)
Async XLA Ops:
  0.0 9.4 %collective-permute-start = (bf16[16,8192]{1,0:T(8,128)(2,1)}, bf16[16,8192]{1,0:T(8,128)(2,1)S(1)}, u32[]{:S(2)}, u32[]{:S(2)}) collective-permute-start(bf16[16,8192]{1,0:T(8,128)(2,1)} %refs_0_.2), channel_id=1, source_target_pairs={{0,5},{1,2},{4,9},{5,0},{8,13},{9,4},{12,15},{13,8},{14,11},{15,12... | collective-permute-start | bytes 786440 | tf_op jit(solution)/shard_map/ppermute | solution.py:261
  2.5 8.0 %collective-permute-start.2 = (bf16[16,8192]{1,0:T(8,128)(2,1)}, bf16[16,8192]{1,0:T(8,128)(2,1)S(1)}, u32[]{:S(2)}, u32[]{:S(2)}) collective-permute-start(bf16[16,8192]{1,0:T(8,128)(2,1)} %refs_0_.2), channel_id=1, source_target_pairs={{1,5},{0,2},{5,9},{4,0},{9,13},{8,4},{13,15},{12,8},{15,11},{14,12... | collective-permute-start | bytes 786440 | tf_op jit(solution)/shard_map/ppermute | solution.py:261
  9.4 5.8 %collective-permute-start.1 = (bf16[16,8192]{1,0:T(8,128)(2,1)S(1)}, bf16[16,8192]{1,0:T(8,128)(2,1)S(1)}, u32[]{:S(2)}, u32[]{:S(2)}) collective-permute-start(bf16[16,8192]{1,0:T(8,128)(2,1)S(1)} %collective-permute-done.refs_0_.refs_1_), channel_id=1, source_target_pairs={{0,3},{1,4},{4,1},{5,8},{8,5},{9,12},{12,9},{13,14},{14,13},{15,10... | collective-permute-start | bytes 786440 | tf_op jit(solution)/shard_map/ppermute | solution.py:261
  10.4 10.0 %collective-permute-start.5 = (bf16[16,8192]{1,0:T(8,128)(2,1)S(1)}, bf16[16,8192]{1,0:T(8,128)(2,1)S(1)}, u32[]{:S(2)}, u32[]{:S(2)}) collective-permute-start(bf16[16,8192]{1,0:T(8,128)(2,1)S(1)} %collective-permute-done.2.refs_1_.refs_2_), channel_id=1, source_target_pairs={{0,3},{1,4},{4,1},{5,8},{8,5},{9,12},{12,9},{13,14},{14,13},{15,10... | collective-permute-start | bytes 786440 | tf_op jit(solution)/shard_map/ppermute | solution.py:261
  15.2 6.4 %collective-permute-start.3 = (bf16[16,8192]{1,0:T(8,128)(2,1)S(1)}, bf16[16,8192]{1,0:T(8,128)(2,1)S(1)}, u32[]{:S(2)}, u32[]{:S(2)}) collective-permute-start(bf16[16,8192]{1,0:T(8,128)(2,1)S(1)} %collective-permute-done.1.refs_0_.refs_3_), channel_id=1, source_target_pairs={{0,5},{1,2},{4,9},{5,0},{8,13},{9,4},{12,15},{13,8},{14,11},{15,12... | collective-permute-start | bytes 786440 | tf_op jit(solution)/shard_map/ppermute | solution.py:261
  17.6 4.9 %copy-start = (bf16[16,8192]{1,0:T(8,128)(2,1)S(1)}, bf16[16,8192]{1,0:T(8,128)(2,1)}, u32[]{:S(2)}) copy-start(bf16[16,8192]{1,0:T(8,128)(2,1)} %refs_0_.2) | copy-start | bytes 786436
  20.5 7.0 %collective-permute-start.6 = (bf16[16,8192]{1,0:T(8,128)(2,1)S(1)}, bf16[16,8192]{1,0:T(8,128)(2,1)S(1)}, u32[]{:S(2)}, u32[]{:S(2)}) collective-permute-start(bf16[16,8192]{1,0:T(8,128)(2,1)S(1)} %collective-permute-done.5.refs_4_), channel_id=1, source_target_pairs={{0,5},{1,2},{4,9},{5,0},{8,13},{9,4},{12,15},{13,8},{14,11},{15,12... | collective-permute-start | bytes 786440 | tf_op jit(solution)/shard_map/ppermute | solution.py:261
  21.7 7.1 %collective-permute-start.4 = (bf16[16,8192]{1,0:T(8,128)(2,1)S(1)}, bf16[16,8192]{1,0:T(8,128)(2,1)S(1)}, u32[]{:S(2)}, u32[]{:S(2)}) collective-permute-start(bf16[16,8192]{1,0:T(8,128)(2,1)S(1)} %collective-permute-done.3.refs_0_.refs_5_), channel_id=1, source_target_pairs={{0,3},{1,4},{4,1},{5,8},{8,5},{9,12},{12,9},{13,14},{14,13},{15,10... | collective-permute-start | bytes 786440 | tf_op jit(solution)/shard_map/ppermute | solution.py:261
  22.6 6.2 %collective-permute-start.7 = (bf16[80,8192]{1,0:T(8,128)(2,1)S(1)}, bf16[80,8192]{1,0:T(8,128)(2,1)S(1)}, u32[]{:S(2)}, u32[]{:S(2)}) collective-permute-start(bf16[80,8192]{1,0:T(8,128)(2,1)S(1)} %shard_map.43), channel_id=1, source_target_pairs={{0,1},{1,0},{4,5},{5,4},{8,9},{9,8},{12,13},{13,12},{14,15},{15,14... | collective-permute-start | bytes 3932168 | tf_op jit(solution)/shard_map/ppermute | solution.py:261
  25.7 3.1 %collective-permute-start.9 = (f32[32,8192]{1,0:T(8,128)S(1)}, f32[32,8192]{1,0:T(8,128)S(1)}, u32[]{:S(2)}, u32[]{:S(2)}) collective-permute-start(f32[32,8192]{1,0:T(8,128)S(1)} %shard_map.44), channel_id=1, source_target_pairs={{0,1},{1,0},{4,5},{5,4},{8,9},{9,8},{12,13},{13,12},{14,15},{15,14... | collective-permute-start | bytes 3145736 | tf_op jit(solution)/shard_map/ppermute | solution.py:261
  25.8 3.0 %collective-permute-start.8 = (bf16[16,8192]{1,0:T(8,128)(2,1)S(1)}, bf16[16,8192]{1,0:T(8,128)(2,1)S(1)}, u32[]{:S(2)}, u32[]{:S(2)}) collective-permute-start(bf16[16,8192]{1,0:T(8,128)(2,1)S(1)} %collective-permute-done.3.refs_0_.refs_5_), channel_id=1, source_target_pairs={{0,1},{1,0},{4,5},{5,4},{8,9},{9,8},{12,13},{13,12},{14,15},{15,14... | collective-permute-start | bytes 786440 | tf_op jit(solution)/shard_map/ppermute | solution.py:261
  29.5 1.2 %collective-permute-start.10 = (f32[1,256]{1,0:T(1,128)S(1)}, f32[1,256]{1,0:T(1,128)S(1)}, u32[]{:S(2)}, u32[]{:S(2)}) collective-permute-start(f32[1,256]{1,0:T(1,128)S(1)} %shard_map.45), channel_id=1, source_target_pairs={{0,1},{1,0},{2,3},{3,2},{4,5},{5,4},{6,7},{7,6},{8,9},{9,8},{10,11... | collective-permute-start | bytes 3080 | tf_op jit(solution)/shard_map/ppermute | solution.py:261
  30.7 3.0 %collective-permute-start.11 = (f32[1,256]{1,0:T(1,128)S(1)}, f32[1,256]{1,0:T(1,128)S(1)}, u32[]{:S(2)}, u32[]{:S(2)}) collective-permute-start(f32[1,256]{1,0:T(1,128)S(1)} %add.15), channel_id=1, source_target_pairs={{0,5},{1,4},{2,7},{3,6},{4,1},{5,0},{6,3},{7,2},{8,13},{9,12},{10,... | collective-permute-start | bytes 3080 | tf_op jit(solution)/shard_map/ppermute | solution.py:261
  31.9 3.9 %collective-permute-start.12 = (f32[1,256]{1,0:T(1,128)S(1)}, f32[1,256]{1,0:T(1,128)S(1)}, u32[]{:S(2)}, u32[]{:S(2)}) collective-permute-start(f32[1,256]{1,0:T(1,128)S(1)} %add.15), channel_id=1, source_target_pairs={{0,7},{1,6},{2,5},{3,4},{4,3},{5,2},{6,1},{7,0},{8,15},{9,14},{10,... | collective-permute-start | bytes 3080 | tf_op jit(solution)/shard_map/ppermute | solution.py:261
  33.5 3.0 %collective-permute-start.13 = (f32[1,256]{1,0:T(1,128)S(1)}, f32[1,256]{1,0:T(1,128)S(1)}, u32[]{:S(2)}, u32[]{:S(2)}) collective-permute-start(f32[1,256]{1,0:T(1,128)S(1)} %add.15), channel_id=1, source_target_pairs={{0,3},{1,2},{2,1},{3,0},{4,7},{5,6},{6,5},{7,4},{8,11},{9,10},{10,... | collective-permute-start | bytes 3080 | tf_op jit(solution)/shard_map/ppermute | solution.py:261
  36.5 3.9 %collective-permute-start.14 = (f32[1,256]{1,0:T(1,128)S(1)}, f32[1,256]{1,0:T(1,128)S(1)}, u32[]{:S(2)}, u32[]{:S(2)}) collective-permute-start(f32[1,256]{1,0:T(1,128)S(1)} %add_add_fusion), channel_id=1, source_target_pairs={{0,9},{1,8},{2,11},{3,10},{4,13},{5,12},{6,15},{7,14},{8,1},{9,0},... | collective-permute-start | bytes 3080 | tf_op jit(solution)/shard_map/ppermute | solution.py:261
